TPU v7x, 512 devices: a whole 4x8x8 slice. The times are simulated.
512 devices in a mesh: ctx: 32 (over y_hi, z, core), dp: 16 (over x, y_lo).
Axes of the slice: x: 4, y: 8 (y_hi: 2, y_lo: 4; y = y_hi * 4 + y_lo), z: 8, core: 2. Of those that a mesh axis runs over, the one named last changes fastest.
Arguments:
- queries: bfloat16 [16, 2048, 2560], P('dp', 'ctx'), may hold values from -144 to 144
- output_gradient: bfloat16 [16, 2048, 2560], P('dp', 'ctx'), may hold values from -6 to 6
- attention_output: bfloat16 [16, 2048, 2560], P('dp', 'ctx'), may hold values from -3 to 3
- completion_key_rows: bfloat16 [16, 2048, 512], P('dp', 'ctx'), may hold values from -6 to 6
- completion_value_rows: bfloat16 [16, 2048, 512], P('dp', 'ctx'), may hold values from -6 to 6
- prompt_keys: bfloat16 [16, 2048, 512], P('dp', 'ctx'), may hold values from -6 to 6
- prompt_value_rows: bfloat16 [16, 2048, 512], P('dp', 'ctx'), may hold values from -6 to 6
- prompt_states: bfloat16 [16, 2048, 5120], P('dp', None, 'ctx'), may hold values from -6 to 6
- comp_lengths: int32 [16, 32, 4], P('dp', 'ctx'), may hold values from 1 to 32, 64 in all within a row
Outputs:
- grad_query: bfloat16 [16, 2048, 2560], P('dp', 'ctx')
- grad_comp_keys: bfloat16 [16, 2048, 512], P('dp', 'ctx')
- grad_comp_values: bfloat16 [16, 2048, 512], P('dp', 'ctx')
- grad_prompt_keys: bfloat16 [16, 2048, 512], P('dp', 'ctx')
- grad_prompt_values: bfloat16 [16, 2048, 512], P('dp', 'ctx')
- grad_proj: float32 [5120, 512], P('ctx', 'dp')
Inputs may be any that keep to these rules, and one draw needn't show every extreme that they name: `comp_lengths`: the 4 lengths of one device sum to 64.
All inputs are finite; a program needn't handle non-finite values.
Results may differ from a plain program's by a relative error of at most 0.0051.
Values may be sent and summed in bfloat16 or wider, within the bound.
A program may use at most 128 MiB of HBM per device.

v0:
```python
import jax
import jax.numpy as jnp
from jax import lax
from jax.sharding import PartitionSpec as P

QUERY_HEAD_COUNT = 20
KEY_HEAD_COUNT = 4
HEAD_SIZE = 128


MASKED = -1e30


def passed_along(value, axis, steps):
    count = lax.axis_size(axis)
    pairs = [(source, (source + steps) % count) for source in range(count)]
    return lax.ppermute(value, axis, pairs)


def visible_mask(token_lengths, local_rows):
    slot_ends = jnp.cumsum(token_lengths)
    position = jnp.arange(local_rows, dtype=jnp.int32)
    segment = jnp.sum((position[:, None] >= slot_ends[None, :]).astype(jnp.int32), axis=1)
    return (segment[:, None] == segment[None, :]) & (position[None, :] <= position[:, None])


def by_head(block_of_rows):
    return block_of_rows.reshape(block_of_rows.shape[0], KEY_HEAD_COUNT, HEAD_SIZE)


def head_scores(heads_of_query, heads_of_key):
    products = jnp.einsum(
        "chgd,khd->chgk", heads_of_query, heads_of_key, preferred_element_type=jnp.float32
    )
    return products * HEAD_SIZE ** (-0.5)


def merge_stats(stats_now, scores):
    running_top, running_sum = stats_now
    new_top = jnp.maximum(running_top, jnp.max(scores, axis=-1))
    running_sum = running_sum * jnp.exp(running_top - new_top) + jnp.sum(
        jnp.exp(scores - new_top[..., None]), axis=-1
    )
    return (new_top, running_sum)


def key_grads(
    heads_of_query, cotangent_by_head, log_total, row_delta, heads_of_key, heads_of_value, seen_mask
):
    scores = head_scores(heads_of_query, heads_of_key)
    if seen_mask is not None:
        scores = jnp.where(seen_mask[:, None, None, :], scores, MASKED)
    softmax_p = jnp.exp(scores - log_total[..., None])
    dprobs = jnp.einsum(
        "chgd,khd->chgk", cotangent_by_head, heads_of_value, preferred_element_type=jnp.float32
    )
    dscores = softmax_p * (dprobs - row_delta[..., None])
    probs_bf = softmax_p.astype(jnp.bfloat16)
    dscores_bf = dscores.astype(jnp.bfloat16)
    query_gradient = jnp.einsum(
        "chgk,khd->chgd", dscores_bf, heads_of_key, preferred_element_type=jnp.float32
    ) * HEAD_SIZE ** (-0.5)
    key_gradient = jnp.einsum(
        "chgk,chgd->khd", dscores_bf, heads_of_query, preferred_element_type=jnp.float32
    ) * HEAD_SIZE ** (-0.5)
    value_gradient = jnp.einsum(
        "chgk,chgd->khd", probs_bf, cotangent_by_head, preferred_element_type=jnp.float32
    )
    return (query_gradient, key_gradient, value_gradient)


def prompt_pass(term_at, advance, values_start, query_shape, key_value_width):

    def cycle_step(step_index, cycle_state):
        values_now, key_sum, value_sum, query_sum = cycle_state
        query_gradient, key_gradient, value_gradient = term_at(step_index, values_now)
        key_sum = key_sum + key_gradient.reshape(-1, key_value_width)
        value_sum = value_sum + value_gradient.reshape(-1, key_value_width)
        values_now = advance(values_now)
        key_sum, value_sum = passed_along((key_sum, value_sum), "ctx", 1)
        return (values_now, key_sum, value_sum, query_sum + query_gradient)

    last_step = lax.axis_size("ctx") - 1
    zero_rows = jnp.zeros((values_start.shape[0], key_value_width), jnp.float32)
    cycle_start = (values_start, zero_rows, zero_rows, jnp.zeros(query_shape, jnp.float32))
    values_now, key_sum, value_sum, query_sum = lax.fori_loop(0, last_step, cycle_step, cycle_start)
    query_gradient, key_gradient, value_gradient = term_at(jnp.int32(last_step), values_now)
    owned_k, owned_v = passed_along(
        (
            key_sum + key_gradient.reshape(-1, key_value_width),
            value_sum + value_gradient.reshape(-1, key_value_width),
        ),
        "ctx",
        1,
    )
    return (owned_k, owned_v, query_sum + query_gradient)


def body(
    queries,
    output_gradient,
    attention_output,
    completion_key_rows,
    completion_value_rows,
    prompt_keys,
    prompt_value_rows,
    prompt_states,
    comp_lengths,
):
    local_rows = queries.shape[1]
    group_length = QUERY_HEAD_COUNT // KEY_HEAD_COUNT
    key_value_width = KEY_HEAD_COUNT * HEAD_SIZE
    shard_rows = prompt_keys.shape[1]
    cycle_size = lax.axis_size("ctx")
    my_index = lax.axis_index("ctx")
    heads_of_query = queries[0].reshape(local_rows, KEY_HEAD_COUNT, group_length, HEAD_SIZE)
    cotangent_by_head = output_gradient[0].reshape(
        local_rows, KEY_HEAD_COUNT, group_length, HEAD_SIZE
    )
    saved_by_head = attention_output[0].reshape(local_rows, KEY_HEAD_COUNT, group_length, HEAD_SIZE)
    row_delta = jnp.einsum(
        "chgd,chgd->chg", cotangent_by_head, saved_by_head, preferred_element_type=jnp.float32
    )
    own_keys = by_head(completion_key_rows[0])
    own_values = by_head(completion_value_rows[0])
    seen_mask = visible_mask(comp_lengths[0, 0], local_rows)
    self_scores = jnp.where(
        seen_mask[:, None, None, :], head_scores(heads_of_query, own_keys), MASKED
    )
    prompt_key_block = prompt_keys[0]
    prompt_value_block = prompt_value_rows[0]
    all_keys = lax.all_gather(prompt_key_block, "ctx", axis=0, tiled=True)
    key_heads_all = by_head(all_keys)
    top_parts = []
    sum_parts = []
    for index_of_head in range(KEY_HEAD_COUNT):
        head_cut = slice(index_of_head, index_of_head + 1)
        start_stats = (
            jnp.full((local_rows, 1, group_length), MASKED, jnp.float32),
            jnp.zeros((local_rows, 1, group_length), jnp.float32),
        )
        head_top, head_sum = merge_stats(
            start_stats, head_scores(heads_of_query[:, head_cut], key_heads_all[:, head_cut])
        )
        top_parts.append(head_top)
        sum_parts.append(head_sum)
    prompt_stats = (jnp.concatenate(top_parts, axis=1), jnp.concatenate(sum_parts, axis=1))
    running_top, running_sum = merge_stats(prompt_stats, self_scores)
    log_total = running_top + jnp.log(running_sum)

    def shard_of(step_index):
        return lax.rem(my_index - step_index.astype(jnp.int32) + cycle_size, cycle_size)

    def keys_at(step_index):
        return lax.dynamic_slice_in_dim(all_keys, shard_of(step_index) * shard_rows, shard_rows, 0)

    def term_at(step_index, values_now):
        return key_grads(
            heads_of_query,
            cotangent_by_head,
            log_total,
            row_delta,
            by_head(keys_at(step_index)),
            by_head(values_now),
            None,
        )

    def advance(values_now):
        return passed_along(values_now, "ctx", 1)

    owned_k, owned_v, prompt_query = prompt_pass(
        term_at, advance, prompt_value_block, heads_of_query.shape, key_value_width
    )
    self_q, self_k, self_v = key_grads(
        heads_of_query, cotangent_by_head, log_total, row_delta, own_keys, own_values, seen_mask
    )
    grad_query = (
        (prompt_query + self_q)
        .reshape(local_rows, QUERY_HEAD_COUNT * HEAD_SIZE)
        .astype(jnp.bfloat16)[None]
    )
    grad_comp_keys = self_k.reshape(local_rows, key_value_width).astype(jnp.bfloat16)[None]
    grad_comp_values = self_v.reshape(local_rows, key_value_width).astype(jnp.bfloat16)[None]
    prompt_gk = owned_k.astype(jnp.bfloat16)
    prompt_gv = owned_v.astype(jnp.bfloat16)
    every_row = lax.all_gather(prompt_gk, "ctx", axis=0, tiled=True)
    partial_proj = jnp.einsum(
        "pd,pk->dk", prompt_states[0], every_row, preferred_element_type=jnp.float32
    )
    grad_proj = lax.psum_scatter(partial_proj, "dp", scatter_dimension=1, tiled=True)
    return (
        grad_query,
        grad_comp_keys,
        grad_comp_values,
        prompt_gk[None],
        prompt_gv[None],
        grad_proj,
    )


def solution(mesh):
    in_specs = (
        P("dp", "ctx", None),
        P("dp", "ctx", None),
        P("dp", "ctx", None),
        P("dp", "ctx", None),
        P("dp", "ctx", None),
        P("dp", "ctx", None),
        P("dp", "ctx", None),
        P("dp", None, "ctx"),
        P("dp", "ctx", None),
    )
    out_specs = (
        P("dp", "ctx", None),
        P("dp", "ctx", None),
        P("dp", "ctx", None),
        P("dp", "ctx", None),
        P("dp", "ctx", None),
        P("ctx", "dp"),
    )
    return jax.shard_map(body, mesh=mesh, in_specs=in_specs, out_specs=out_specs, check_vma=False)
```

profile of v0, /device:TPU:1, one launch (start us, length us, event | category | flops | bytes accessed | tf_op | source)
XLA Modules:
  0.0 965.0 jit_solution(1053463703863508371)
XLA Ops:
  16.7 90.9 %all-gather.6.cloned.1.call-done = bf16[1,2048,512]{2,1,0:T(8,128)(2,1)} async-done(((bf16[1,64,512]{2,1,0:T(8,128)(2,1)}), bf16[1,2048,512]{2,1,0:T(8,128)(2,1)}) %all-gather.6.cloned.1.call-update) | async-done | bytes 2097168 | tf_op jit(solution)/shard_map/all_gather | solution.py:132
  107.7 4.0 copy.110
  111.6 3.2 fusion.64
  127.6 645.5 %while.20 = (s32[]{:T(128)}, bf16[64,512]{1,0:T(8,128)(2,1)}, f32[64,512]{1,0:T(8,128)S(1)}, f32[64,512]{1,0:T(8,128)S(1)}, f32[64,4,5,128]{3,0,2,1:T(8,128)S(1)...) while((s32[]{:T(128)}, bf16[64,512]{1,0:T(8,128)(2,1)}, ...), condition=%wide.region_13.14_spmd.clone, body=%wide.region_12.13_spmd.clone.sunk | while | flops 105938960 | bytes 7186856 | solution.py:86
  128.5 3.4 collective-permute-start
  142.8 4.2 collective-permute-start
  152.7 4.0 collective-permute-start.2
  157.1 3.1 collective-permute-done.1
  174.0 4.6 collective-permute-done
  178.5 4.6 collective-permute-done.1
  197.0 3.2 collective-permute-done
  200.2 4.6 collective-permute-done.1
  221.5 4.6 collective-permute-done.1
  242.7 4.6 collective-permute-done.1
  263.9 4.6 collective-permute-done.1
  284.9 4.6 collective-permute-done.1
  289.5 3.1 collective-permute-done.2
  305.8 4.6 collective-permute-done.1
  310.4 3.1 collective-permute-done.2
  326.7 4.6 collective-permute-done.1
  331.3 3.1 collective-permute-done.2
  347.6 4.6 collective-permute-done.1
  352.2 3.1 collective-permute-done.2
  368.5 4.6 collective-permute-done.1
  373.1 3.1 collective-permute-done.2
  389.4 4.6 collective-permute-done.1
  394.0 3.1 collective-permute-done.2
  410.2 4.6 collective-permute-done.1
  431.1 4.6 collective-permute-done.1
  452.0 4.6 collective-permute-done.1
  472.9 4.6 collective-permute-done.1
  493.8 4.6 collective-permute-done.1
  514.7 4.6 collective-permute-done.1
  535.6 4.6 collective-permute-done.1
  556.5 4.6 collective-permute-done.1
  577.4 4.6 collective-permute-done.1
  598.3 4.6 collective-permute-done.1
  619.2 4.6 collective-permute-done.1
  640.1 4.6 collective-permute-done.1
  661.0 4.6 collective-permute-done.1
  681.8 4.6 collective-permute-done.1
  702.7 4.6 collective-permute-done.1
  723.6 4.6 collective-permute-done.1
  744.5 4.6 collective-permute-done.1
  765.4 4.6 collective-permute-done.1
  779.8 10.3 %collective-permute-done.3 = bf16[64,512]{1,0:T(8,128)(2,1)S(1)} collective-permute-done((bf16[64,512]{1,0:T(8,128)(2,1)S(1)}, bf16[64,512]{1,0:T(8,128)(2,1)S(1)}, u32[]{:S(2)}, u32[]{:S(2)}) %collective-permute-start.3) | collective-permute-done | bytes 65568 | tf_op jit(solution)/shard_map/ppermute | solution.py:17
  798.5 82.4 %all-gather.4.cloned.1.call-done = bf16[2048,512]{1,0:T(8,128)(2,1)} async-done(((bf16[64,512]{1,0:T(8,128)(2,1)}), bf16[2048,512]{1,0:T(8,128)(2,1)}) %all-gather.4.cloned.1.call-update) | async-done | bytes 2097168 | tf_op jit(solution)/shard_map/all_gather | solution.py:186
  887.7 68.7 %reduce-scatter.4.cloned.1.call-done = f32[32,160]{1,0:T(8,128)} async-done(((f32[512,160]{1,0:T(8,128)}), f32[32,160]{1,0:T(8,128)}) %reduce-scatter.4.cloned.1.call-update) | async-done | bytes 20496
  (576 shorter events, 512.7 us)
Async XLA Ops:
  7.2 100.5 %all-gather.6.cloned.1.call-start = ((), (), s32[]{:S(2)}) async-start(), calls=%async_computation.2 | async-start | bytes 2162688 | tf_op jit(solution)/shard_map/all_gather | solution.py:132
  8.8 872.1 %all-gather.4.cloned.1.call-start = ((), (), s32[]{:S(2)}) async-start(), calls=%async_computation.1 | async-start | bytes 2162688 | tf_op jit(solution)/shard_map/all_gather | solution.py:186
  142.8 14.3 %collective-permute-start = (bf16[64,512]{1,0:T(8,128)(2,1)S(1)}, bf16[64,512]{1,0:T(8,128)(2,1)}, u32[]{:S(2)}, u32[]{:S(2)}) collective-permute-start(bf16[64,512]{1,0:T(8,128)(2,1)S(1)} %copy.235), channel_id=1, source_target_pairs={{0,16},{16,32},{32,48},{48,64},{64,80},{80,96},{96,112},{112,128},... | collective-permute-start | bytes 196616 | tf_op jit(solution)/shard_map/while/body/eval_jaxpr/ppermute | solution.py:17
  164.1 14.4 %collective-permute-start = (bf16[64,512]{1,0:T(8,128)(2,1)S(1)}, bf16[64,512]{1,0:T(8,128)(2,1)}, u32[]{:S(2)}, u32[]{:S(2)}) collective-permute-start(bf16[64,512]{1,0:T(8,128)(2,1)S(1)} %copy.235), channel_id=1, source_target_pairs={{0,16},{16,32},{32,48},{48,64},{64,80},{80,96},{96,112},{112,128},... | collective-permute-start | bytes 196616 | tf_op jit(solution)/shard_map/while/body/eval_jaxpr/ppermute | solution.py:17
  168.8 14.4 %collective-permute-start.1 = (f32[64,512]{1,0:T(8,128)S(1)}, f32[64,512]{1,0:T(8,128)S(1)}, u32[]{:S(2)}, u32[]{:S(2)}) collective-permute-start(f32[64,512]{1,0:T(8,128)S(1)} %bitcast_add_fusion.10), channel_id=1, source_target_pairs={{0,16},{16,32},{32,48},{48,64},{64,80},{80,96},{96,112},{112,128},... | collective-permute-start | bytes 393224 | tf_op jit(solution)/shard_map/while/body/eval_jaxpr/ppermute | solution.py:17
  171.7 14.6 %collective-permute-start.2 = (f32[64,512]{1,0:T(8,128)}, f32[64,512]{1,0:T(8,128)S(1)}, u32[]{:S(2)}, u32[]{:S(2)}) collective-permute-start(f32[64,512]{1,0:T(8,128)} %bitcast_add_fusion.11), channel_id=1, source_target_pairs={{0,16},{16,32},{32,48},{48,64},{64,80},{80,96},{96,112},{112,128},... | collective-permute-start | bytes 393224 | tf_op jit(solution)/shard_map/while/body/eval_jaxpr/ppermute | solution.py:17
  187.1 13.1 %collective-permute-start = (bf16[64,512]{1,0:T(8,128)(2,1)S(1)}, bf16[64,512]{1,0:T(8,128)(2,1)}, u32[]{:S(2)}, u32[]{:S(2)}) collective-permute-start(bf16[64,512]{1,0:T(8,128)(2,1)S(1)} %copy.235), channel_id=1, source_target_pairs={{0,16},{16,32},{32,48},{48,64},{64,80},{80,96},{96,112},{112,128},... | collective-permute-start | bytes 196616 | tf_op jit(solution)/shard_map/while/body/eval_jaxpr/ppermute | solution.py:17
  191.8 13.1 %collective-permute-start.1 = (f32[64,512]{1,0:T(8,128)S(1)}, f32[64,512]{1,0:T(8,128)S(1)}, u32[]{:S(2)}, u32[]{:S(2)}) collective-permute-start(f32[64,512]{1,0:T(8,128)S(1)} %bitcast_add_fusion.10), channel_id=1, source_target_pairs={{0,16},{16,32},{32,48},{48,64},{64,80},{80,96},{96,112},{112,128},... | collective-permute-start | bytes 393224 | tf_op jit(solution)/shard_map/while/body/eval_jaxpr/ppermute | solution.py:17
  194.7 13.2 %collective-permute-start.2 = (f32[64,512]{1,0:T(8,128)}, f32[64,512]{1,0:T(8,128)S(1)}, u32[]{:S(2)}, u32[]{:S(2)}) collective-permute-start(f32[64,512]{1,0:T(8,128)} %bitcast_add_fusion.11), channel_id=1, source_target_pairs={{0,16},{16,32},{32,48},{48,64},{64,80},{80,96},{96,112},{112,128},... | collective-permute-start | bytes 393224 | tf_op jit(solution)/shard_map/while/body/eval_jaxpr/ppermute | solution.py:17
  208.8 12.8 %collective-permute-start = (bf16[64,512]{1,0:T(8,128)(2,1)S(1)}, bf16[64,512]{1,0:T(8,128)(2,1)}, u32[]{:S(2)}, u32[]{:S(2)}) collective-permute-start(bf16[64,512]{1,0:T(8,128)(2,1)S(1)} %copy.235), channel_id=1, source_target_pairs={{0,16},{16,32},{32,48},{48,64},{64,80},{80,96},{96,112},{112,128},... | collective-permute-start | bytes 196616 | tf_op jit(solution)/shard_map/while/body/eval_jaxpr/ppermute | solution.py:17
  213.4 12.7 %collective-permute-start.1 = (f32[64,512]{1,0:T(8,128)S(1)}, f32[64,512]{1,0:T(8,128)S(1)}, u32[]{:S(2)}, u32[]{:S(2)}) collective-permute-start(f32[64,512]{1,0:T(8,128)S(1)} %bitcast_add_fusion.10), channel_id=1, source_target_pairs={{0,16},{16,32},{32,48},{48,64},{64,80},{80,96},{96,112},{112,128},... | collective-permute-start | bytes 393224 | tf_op jit(solution)/shard_map/while/body/eval_jaxpr/ppermute | solution.py:17
  216.3 12.9 %collective-permute-start.2 = (f32[64,512]{1,0:T(8,128)}, f32[64,512]{1,0:T(8,128)S(1)}, u32[]{:S(2)}, u32[]{:S(2)}) collective-permute-start(f32[64,512]{1,0:T(8,128)} %bitcast_add_fusion.11), channel_id=1, source_target_pairs={{0,16},{16,32},{32,48},{48,64},{64,80},{80,96},{96,112},{112,128},... | collective-permute-start | bytes 393224 | tf_op jit(solution)/shard_map/while/body/eval_jaxpr/ppermute | solution.py:17
  230.1 12.7 %collective-permute-start = (bf16[64,512]{1,0:T(8,128)(2,1)S(1)}, bf16[64,512]{1,0:T(8,128)(2,1)}, u32[]{:S(2)}, u32[]{:S(2)}) collective-permute-start(bf16[64,512]{1,0:T(8,128)(2,1)S(1)} %copy.235), channel_id=1, source_target_pairs={{0,16},{16,32},{32,48},{48,64},{64,80},{80,96},{96,112},{112,128},... | collective-permute-start | bytes 196616 | tf_op jit(solution)/shard_map/while/body/eval_jaxpr/ppermute | solution.py:17
  234.8 12.6 %collective-permute-start.1 = (f32[64,512]{1,0:T(8,128)S(1)}, f32[64,512]{1,0:T(8,128)S(1)}, u32[]{:S(2)}, u32[]{:S(2)}) collective-permute-start(f32[64,512]{1,0:T(8,128)S(1)} %bitcast_add_fusion.10), channel_id=1, source_target_pairs={{0,16},{16,32},{32,48},{48,64},{64,80},{80,96},{96,112},{112,128},... | collective-permute-start | bytes 393224 | tf_op jit(solution)/shard_map/while/body/eval_jaxpr/ppermute | solution.py:17
  237.6 12.8 %collective-permute-start.2 = (f32[64,512]{1,0:T(8,128)}, f32[64,512]{1,0:T(8,128)S(1)}, u32[]{:S(2)}, u32[]{:S(2)}) collective-permute-start(f32[64,512]{1,0:T(8,128)} %bitcast_add_fusion.11), channel_id=1, source_target_pairs={{0,16},{16,32},{32,48},{48,64},{64,80},{80,96},{96,112},{112,128},... | collective-permute-start | bytes 393224 | tf_op jit(solution)/shard_map/while/body/eval_jaxpr/ppermute | solution.py:17
  251.3 12.6 %collective-permute-start = (bf16[64,512]{1,0:T(8,128)(2,1)S(1)}, bf16[64,512]{1,0:T(8,128)(2,1)}, u32[]{:S(2)}, u32[]{:S(2)}) collective-permute-start(bf16[64,512]{1,0:T(8,128)(2,1)S(1)} %copy.235), channel_id=1, source_target_pairs={{0,16},{16,32},{32,48},{48,64},{64,80},{80,96},{96,112},{112,128},... | collective-permute-start | bytes 196616 | tf_op jit(solution)/shard_map/while/body/eval_jaxpr/ppermute | solution.py:17
  256.0 12.5 %collective-permute-start.1 = (f32[64,512]{1,0:T(8,128)S(1)}, f32[64,512]{1,0:T(8,128)S(1)}, u32[]{:S(2)}, u32[]{:S(2)}) collective-permute-start(f32[64,512]{1,0:T(8,128)S(1)} %bitcast_add_fusion.10), channel_id=1, source_target_pairs={{0,16},{16,32},{32,48},{48,64},{64,80},{80,96},{96,112},{112,128},... | collective-permute-start | bytes 393224 | tf_op jit(solution)/shard_map/while/body/eval_jaxpr/ppermute | solution.py:17
  258.9 12.7 %collective-permute-start.2 = (f32[64,512]{1,0:T(8,128)}, f32[64,512]{1,0:T(8,128)S(1)}, u32[]{:S(2)}, u32[]{:S(2)}) collective-permute-start(f32[64,512]{1,0:T(8,128)} %bitcast_add_fusion.11), channel_id=1, source_target_pairs={{0,16},{16,32},{32,48},{48,64},{64,80},{80,96},{96,112},{112,128},... | collective-permute-start | bytes 393224 | tf_op jit(solution)/shard_map/while/body/eval_jaxpr/ppermute | solution.py:17
  272.4 12.5 %collective-permute-start = (bf16[64,512]{1,0:T(8,128)(2,1)S(1)}, bf16[64,512]{1,0:T(8,128)(2,1)}, u32[]{:S(2)}, u32[]{:S(2)}) collective-permute-start(bf16[64,512]{1,0:T(8,128)(2,1)S(1)} %copy.235), channel_id=1, source_target_pairs={{0,16},{16,32},{32,48},{48,64},{64,80},{80,96},{96,112},{112,128},... | collective-permute-start | bytes 196616 | tf_op jit(solution)/shard_map/while/body/eval_jaxpr/ppermute | solution.py:17
  277.1 12.4 %collective-permute-start.1 = (f32[64,512]{1,0:T(8,128)S(1)}, f32[64,512]{1,0:T(8,128)S(1)}, u32[]{:S(2)}, u32[]{:S(2)}) collective-permute-start(f32[64,512]{1,0:T(8,128)S(1)} %bitcast_add_fusion.10), channel_id=1, source_target_pairs={{0,16},{16,32},{32,48},{48,64},{64,80},{80,96},{96,112},{112,128},... | collective-permute-start | bytes 393224 | tf_op jit(solution)/shard_map/while/body/eval_jaxpr/ppermute | solution.py:17
  280.0 12.6 %collective-permute-start.2 = (f32[64,512]{1,0:T(8,128)}, f32[64,512]{1,0:T(8,128)S(1)}, u32[]{:S(2)}, u32[]{:S(2)}) collective-permute-start(f32[64,512]{1,0:T(8,128)} %bitcast_add_fusion.11), channel_id=1, source_target_pairs={{0,16},{16,32},{32,48},{48,64},{64,80},{80,96},{96,112},{112,128},... | collective-permute-start | bytes 393224 | tf_op jit(solution)/shard_map/while/body/eval_jaxpr/ppermute | solution.py:17
  293.4 12.3 %collective-permute-start = (bf16[64,512]{1,0:T(8,128)(2,1)S(1)}, bf16[64,512]{1,0:T(8,128)(2,1)}, u32[]{:S(2)}, u32[]{:S(2)}) collective-permute-start(bf16[64,512]{1,0:T(8,128)(2,1)S(1)} %copy.235), channel_id=1, source_target_pairs={{0,16},{16,32},{32,48},{48,64},{64,80},{80,96},{96,112},{112,128},... | collective-permute-start | bytes 196616 | tf_op jit(solution)/shard_map/while/body/eval_jaxpr/ppermute | solution.py:17
  301.0 12.5 %collective-permute-start.2 = (f32[64,512]{1,0:T(8,128)}, f32[64,512]{1,0:T(8,128)S(1)}, u32[]{:S(2)}, u32[]{:S(2)}) collective-permute-start(f32[64,512]{1,0:T(8,128)} %bitcast_add_fusion.11), channel_id=1, source_target_pairs={{0,16},{16,32},{32,48},{48,64},{64,80},{80,96},{96,112},{112,128},... | collective-permute-start | bytes 393224 | tf_op jit(solution)/shard_map/while/body/eval_jaxpr/ppermute | solution.py:17
  321.9 12.5 %collective-permute-start.2 = (f32[64,512]{1,0:T(8,128)}, f32[64,512]{1,0:T(8,128)S(1)}, u32[]{:S(2)}, u32[]{:S(2)}) collective-permute-start(f32[64,512]{1,0:T(8,128)} %bitcast_add_fusion.11), channel_id=1, source_target_pairs={{0,16},{16,32},{32,48},{48,64},{64,80},{80,96},{96,112},{112,128},... | collective-permute-start | bytes 393224 | tf_op jit(solution)/shard_map/while/body/eval_jaxpr/ppermute | solution.py:17
  335.2 12.3 %collective-permute-start = (bf16[64,512]{1,0:T(8,128)(2,1)S(1)}, bf16[64,512]{1,0:T(8,128)(2,1)}, u32[]{:S(2)}, u32[]{:S(2)}) collective-permute-start(bf16[64,512]{1,0:T(8,128)(2,1)S(1)} %copy.235), channel_id=1, source_target_pairs={{0,16},{16,32},{32,48},{48,64},{64,80},{80,96},{96,112},{112,128},... | collective-permute-start | bytes 196616 | tf_op jit(solution)/shard_map/while/body/eval_jaxpr/ppermute | solution.py:17
  342.8 12.5 %collective-permute-start.2 = (f32[64,512]{1,0:T(8,128)}, f32[64,512]{1,0:T(8,128)S(1)}, u32[]{:S(2)}, u32[]{:S(2)}) collective-permute-start(f32[64,512]{1,0:T(8,128)} %bitcast_add_fusion.11), channel_id=1, source_target_pairs={{0,16},{16,32},{32,48},{48,64},{64,80},{80,96},{96,112},{112,128},... | collective-permute-start | bytes 393224 | tf_op jit(solution)/shard_map/while/body/eval_jaxpr/ppermute | solution.py:17
  363.7 12.5 %collective-permute-start.2 = (f32[64,512]{1,0:T(8,128)}, f32[64,512]{1,0:T(8,128)S(1)}, u32[]{:S(2)}, u32[]{:S(2)}) collective-permute-start(f32[64,512]{1,0:T(8,128)} %bitcast_add_fusion.11), channel_id=1, source_target_pairs={{0,16},{16,32},{32,48},{48,64},{64,80},{80,96},{96,112},{112,128},... | collective-permute-start | bytes 393224 | tf_op jit(solution)/shard_map/while/body/eval_jaxpr/ppermute | solution.py:17
  384.6 12.5 %collective-permute-start.2 = (f32[64,512]{1,0:T(8,128)}, f32[64,512]{1,0:T(8,128)S(1)}, u32[]{:S(2)}, u32[]{:S(2)}) collective-permute-start(f32[64,512]{1,0:T(8,128)} %bitcast_add_fusion.11), channel_id=1, source_target_pairs={{0,16},{16,32},{32,48},{48,64},{64,80},{80,96},{96,112},{112,128},... | collective-permute-start | bytes 393224 | tf_op jit(solution)/shard_map/while/body/eval_jaxpr/ppermute | solution.py:17
  405.5 12.5 %collective-permute-start.2 = (f32[64,512]{1,0:T(8,128)}, f32[64,512]{1,0:T(8,128)S(1)}, u32[]{:S(2)}, u32[]{:S(2)}) collective-permute-start(f32[64,512]{1,0:T(8,128)} %bitcast_add_fusion.11), channel_id=1, source_target_pairs={{0,16},{16,32},{32,48},{48,64},{64,80},{80,96},{96,112},{112,128},... | collective-permute-start | bytes 393224 | tf_op jit(solution)/shard_map/while/body/eval_jaxpr/ppermute | solution.py:17
  426.4 12.5 %collective-permute-start.2 = (f32[64,512]{1,0:T(8,128)}, f32[64,512]{1,0:T(8,128)S(1)}, u32[]{:S(2)}, u32[]{:S(2)}) collective-permute-start(f32[64,512]{1,0:T(8,128)} %bitcast_add_fusion.11), channel_id=1, source_target_pairs={{0,16},{16,32},{32,48},{48,64},{64,80},{80,96},{96,112},{112,128},... | collective-permute-start | bytes 393224 | tf_op jit(solution)/shard_map/while/body/eval_jaxpr/ppermute | solution.py:17
  447.2 12.5 %collective-permute-start.2 = (f32[64,512]{1,0:T(8,128)}, f32[64,512]{1,0:T(8,128)S(1)}, u32[]{:S(2)}, u32[]{:S(2)}) collective-permute-start(f32[64,512]{1,0:T(8,128)} %bitcast_add_fusion.11), channel_id=1, source_target_pairs={{0,16},{16,32},{32,48},{48,64},{64,80},{80,96},{96,112},{112,128},... | collective-permute-start | bytes 393224 | tf_op jit(solution)/shard_map/while/body/eval_jaxpr/ppermute | solution.py:17
  468.1 12.5 %collective-permute-start.2 = (f32[64,512]{1,0:T(8,128)}, f32[64,512]{1,0:T(8,128)S(1)}, u32[]{:S(2)}, u32[]{:S(2)}) collective-permute-start(f32[64,512]{1,0:T(8,128)} %bitcast_add_fusion.11), channel_id=1, source_target_pairs={{0,16},{16,32},{32,48},{48,64},{64,80},{80,96},{96,112},{112,128},... | collective-permute-start | bytes 393224 | tf_op jit(solution)/shard_map/while/body/eval_jaxpr/ppermute | solution.py:17
  489.0 12.5 %collective-permute-start.2 = (f32[64,512]{1,0:T(8,128)}, f32[64,512]{1,0:T(8,128)S(1)}, u32[]{:S(2)}, u32[]{:S(2)}) collective-permute-start(f32[64,512]{1,0:T(8,128)} %bitcast_add_fusion.11), channel_id=1, source_target_pairs={{0,16},{16,32},{32,48},{48,64},{64,80},{80,96},{96,112},{112,128},... | collective-permute-start | bytes 393224 | tf_op jit(solution)/shard_map/while/body/eval_jaxpr/ppermute | solution.py:17
  509.9 12.5 %collective-permute-start.2 = (f32[64,512]{1,0:T(8,128)}, f32[64,512]{1,0:T(8,128)S(1)}, u32[]{:S(2)}, u32[]{:S(2)}) collective-permute-start(f32[64,512]{1,0:T(8,128)} %bitcast_add_fusion.11), channel_id=1, source_target_pairs={{0,16},{16,32},{32,48},{48,64},{64,80},{80,96},{96,112},{112,128},... | collective-permute-start | bytes 393224 | tf_op jit(solution)/shard_map/while/body/eval_jaxpr/ppermute | solution.py:17
  530.8 12.5 %collective-permute-start.2 = (f32[64,512]{1,0:T(8,128)}, f32[64,512]{1,0:T(8,128)S(1)}, u32[]{:S(2)}, u32[]{:S(2)}) collective-permute-start(f32[64,512]{1,0:T(8,128)} %bitcast_add_fusion.11), channel_id=1, source_target_pairs={{0,16},{16,32},{32,48},{48,64},{64,80},{80,96},{96,112},{112,128},... | collective-permute-start | bytes 393224 | tf_op jit(solution)/shard_map/while/body/eval_jaxpr/ppermute | solution.py:17
  551.7 12.5 %collective-permute-start.2 = (f32[64,512]{1,0:T(8,128)}, f32[64,512]{1,0:T(8,128)S(1)}, u32[]{:S(2)}, u32[]{:S(2)}) collective-permute-start(f32[64,512]{1,0:T(8,128)} %bitcast_add_fusion.11), channel_id=1, source_target_pairs={{0,16},{16,32},{32,48},{48,64},{64,80},{80,96},{96,112},{112,128},... | collective-permute-start | bytes 393224 | tf_op jit(solution)/shard_map/while/body/eval_jaxpr/ppermute | solution.py:17
  572.6 12.5 %collective-permute-start.2 = (f32[64,512]{1,0:T(8,128)}, f32[64,512]{1,0:T(8,128)S(1)}, u32[]{:S(2)}, u32[]{:S(2)}) collective-permute-start(f32[64,512]{1,0:T(8,128)} %bitcast_add_fusion.11), channel_id=1, source_target_pairs={{0,16},{16,32},{32,48},{48,64},{64,80},{80,96},{96,112},{112,128},... | collective-permute-start | bytes 393224 | tf_op jit(solution)/shard_map/while/body/eval_jaxpr/ppermute | solution.py:17
  593.5 12.5 %collective-permute-start.2 = (f32[64,512]{1,0:T(8,128)}, f32[64,512]{1,0:T(8,128)S(1)}, u32[]{:S(2)}, u32[]{:S(2)}) collective-permute-start(f32[64,512]{1,0:T(8,128)} %bitcast_add_fusion.11), channel_id=1, source_target_pairs={{0,16},{16,32},{32,48},{48,64},{64,80},{80,96},{96,112},{112,128},... | collective-permute-start | bytes 393224 | tf_op jit(solution)/shard_map/while/body/eval_jaxpr/ppermute | solution.py:17
  614.4 12.5 %collective-permute-start.2 = (f32[64,512]{1,0:T(8,128)}, f32[64,512]{1,0:T(8,128)S(1)}, u32[]{:S(2)}, u32[]{:S(2)}) collective-permute-start(f32[64,512]{1,0:T(8,128)} %bitcast_add_fusion.11), channel_id=1, source_target_pairs={{0,16},{16,32},{32,48},{48,64},{64,80},{80,96},{96,112},{112,128},... | collective-permute-start | bytes 393224 | tf_op jit(solution)/shard_map/while/body/eval_jaxpr/ppermute | solution.py:17
  635.3 12.5 %collective-permute-start.2 = (f32[64,512]{1,0:T(8,128)}, f32[64,512]{1,0:T(8,128)S(1)}, u32[]{:S(2)}, u32[]{:S(2)}) collective-permute-start(f32[64,512]{1,0:T(8,128)} %bitcast_add_fusion.11), channel_id=1, source_target_pairs={{0,16},{16,32},{32,48},{48,64},{64,80},{80,96},{96,112},{112,128},... | collective-permute-start | bytes 393224 | tf_op jit(solution)/shard_map/while/body/eval_jaxpr/ppermute | solution.py:17
  656.2 12.5 %collective-permute-start.2 = (f32[64,512]{1,0:T(8,128)}, f32[64,512]{1,0:T(8,128)S(1)}, u32[]{:S(2)}, u32[]{:S(2)}) collective-permute-start(f32[64,512]{1,0:T(8,128)} %bitcast_add_fusion.11), channel_id=1, source_target_pairs={{0,16},{16,32},{32,48},{48,64},{64,80},{80,96},{96,112},{112,128},... | collective-permute-start | bytes 393224 | tf_op jit(solution)/shard_map/while/body/eval_jaxpr/ppermute | solution.py:17
  677.1 12.5 %collective-permute-start.2 = (f32[64,512]{1,0:T(8,128)}, f32[64,512]{1,0:T(8,128)S(1)}, u32[]{:S(2)}, u32[]{:S(2)}) collective-permute-start(f32[64,512]{1,0:T(8,128)} %bitcast_add_fusion.11), channel_id=1, source_target_pairs={{0,16},{16,32},{32,48},{48,64},{64,80},{80,96},{96,112},{112,128},... | collective-permute-start | bytes 393224 | tf_op jit(solution)/shard_map/while/body/eval_jaxpr/ppermute | solution.py:17
  698.0 12.5 %collective-permute-start.2 = (f32[64,512]{1,0:T(8,128)}, f32[64,512]{1,0:T(8,128)S(1)}, u32[]{:S(2)}, u32[]{:S(2)}) collective-permute-start(f32[64,512]{1,0:T(8,128)} %bitcast_add_fusion.11), channel_id=1, source_target_pairs={{0,16},{16,32},{32,48},{48,64},{64,80},{80,96},{96,112},{112,128},... | collective-permute-start | bytes 393224 | tf_op jit(solution)/shard_map/while/body/eval_jaxpr/ppermute | solution.py:17
  718.9 12.5 %collective-permute-start.2 = (f32[64,512]{1,0:T(8,128)}, f32[64,512]{1,0:T(8,128)S(1)}, u32[]{:S(2)}, u32[]{:S(2)}) collective-permute-start(f32[64,512]{1,0:T(8,128)} %bitcast_add_fusion.11), channel_id=1, source_target_pairs={{0,16},{16,32},{32,48},{48,64},{64,80},{80,96},{96,112},{112,128},... | collective-permute-start | bytes 393224 | tf_op jit(solution)/shard_map/while/body/eval_jaxpr/ppermute | solution.py:17
  739.7 12.5 %collective-permute-start.2 = (f32[64,512]{1,0:T(8,128)}, f32[64,512]{1,0:T(8,128)S(1)}, u32[]{:S(2)}, u32[]{:S(2)}) collective-permute-start(f32[64,512]{1,0:T(8,128)} %bitcast_add_fusion.11), channel_id=1, source_target_pairs={{0,16},{16,32},{32,48},{48,64},{64,80},{80,96},{96,112},{112,128},... | collective-permute-start | bytes 393224 | tf_op jit(solution)/shard_map/while/body/eval_jaxpr/ppermute | solution.py:17
  760.6 12.5 %collective-permute-start.2 = (f32[64,512]{1,0:T(8,128)}, f32[64,512]{1,0:T(8,128)S(1)}, u32[]{:S(2)}, u32[]{:S(2)}) collective-permute-start(f32[64,512]{1,0:T(8,128)} %bitcast_add_fusion.11), channel_id=1, source_target_pairs={{0,16},{16,32},{32,48},{48,64},{64,80},{80,96},{96,112},{112,128},... | collective-permute-start | bytes 393224 | tf_op jit(solution)/shard_map/while/body/eval_jaxpr/ppermute | solution.py:17
  790.7 165.7 %reduce-scatter.4.cloned.1.call-start = ((), (), s32[]{:S(2)}) async-start(), calls=%async_computation.3 | async-start | bytes 557056
  793.1 94.5 %collective-permute-start.4 = (bf16[64,512]{1,0:T(8,128)(2,1)}, bf16[64,512]{1,0:T(8,128)(2,1)}, u32[]{:S(2)}, u32[]{:S(2)}) collective-permute-start(bf16[64,512]{1,0:T(8,128)(2,1)} %bitcast_add_fusion.2), channel_id=1, source_target_pairs={{0,16},{16,32},{32,48},{48,64},{64,80},{80,96},{96,112},{112,128},... | collective-permute-start | bytes 196616 | tf_op jit(solution)/shard_map/ppermute | solution.py:17
  (62 other events, 1736.5 us)
Sparse Core Ops, SparseCore 0:
  11.4 96.2 all-gather.5
  790.8 90.0 all-gather.3
  884.3 72.0 reduce-scatter.3
where the time goes:
time: 983 us; the launch traced here: 965 us
  waiting for transfers between devices  560 us (57%)
  starting transfers between devices  188 us (19%)
  matrix products  93.8 us (10%)
  local copies, waits for them, and re-layouts  77.7 us (8%)
  other arithmetic  27.9 us (3%)
  between operations  14 us (1%)
    ppermute x95, waiting for transfers between devices, passed_along(): return lax.ppermute(value, axis, pairs)  318 us
    ppermute x95, starting transfers between devices, passed_along(): return lax.ppermute(value, axis, pairs)  188 us
    all_gather x1, waiting for transfers between devices, body(): all_keys = lax.all_gather(prompt_key_block, 'ctx', axis=0, tiled=True)  90.9 us
    all_gather x1, waiting for transfers between devices, body(): every_row = lax.all_gather(prompt_gk, 'ctx', axis=0, tiled=True)  82.4 us
    unnamed x4, waiting for transfers between devices  68.8 us
    dot_general x33, matrix products, key_grads(): jnp.einsum('chgd,khd->chgk', cotangent_by_head, heads_of_value, preferred...  37.3 us
    dynamic_slice x32, local copies, waits for them, and re-layouts, keys_at(): lax.dynamic_slice_in_dim(all_keys, shard_of(step_index) * shard_rows, sha...  27.2 us
    while x31, local copies, waits for them, and re-layouts  26 us
  transfers between devices with their start and end apart: 98, of which 94 were waited for; matrix products, arithmetic and copies ran while one was open for 15% of the time, Pallas kernels for 0%

commit v1 on v0

v1 whole, which is shorter than its diff:
```python
import functools
import math

import jax
import jax.numpy as jnp
from jax import lax
from jax.experimental import pallas as pl
from jax.experimental.pallas import tpu as pltpu
from jax.sharding import PartitionSpec as P

QUERY_HEAD_COUNT = 20
KEY_HEAD_COUNT = 4
HEAD_SIZE = 128
GROUP = QUERY_HEAD_COUNT // KEY_HEAD_COUNT
MASKED = -1e30
SCALE = HEAD_SIZE ** (-0.5)
LOG2E = math.log2(math.e)
MESH = pl.DeviceIdType.MESH
F32 = jnp.float32
BF16 = jnp.bfloat16

HEADS = KEY_HEAD_COUNT // 2
KW = HEADS * HEAD_SIZE
QW = HEADS * GROUP * HEAD_SIZE
T = 64
ROWS = GROUP * 2 * T
BLOCK = 2 * T


def dot(a, b, ca=1, cb=0):
    return lax.dot_general(a, b, (((ca,), (cb,)), ((), ())), preferred_element_type=F32)


def kernel(
    n_z,
    n_dp,
    q_in,
    do_in,
    o_in,
    kc_in,
    vc_in,
    pk_in,
    pv_in,
    st_in,
    len_in,
    gq_out,
    gkc_out,
    gvc_out,
    gpk_out,
    gpv_out,
    gproj_out,
    kvb,
    raw,
    kvc,
    bias_own,
    bias,
    st,
    qs,
    dos,
    q_t,
    do_t,
    delta,
    top,
    total,
    sbuf,
    sc,
    dq_t,
    part,
    sb,
    rb,
    yb,
    dkb,
    dvf,
    proj,
    prx,
    gqs,
    gkvc,
    loc,
    sib_s,
    sib_r,
    y_s,
    y_r,
    kv_s,
    kv_r,
    rs_s,
    rs_r,
    dk_s,
    dk_r,
    pj_s,
    pj_r,
    ret_s,
    ret_r,
):
    half = n_z // 2
    per_core = n_dp // 2
    cols = KEY_HEAD_COUNT * HEAD_SIZE // n_dp
    c = lax.axis_index("ctx")
    g = lax.axis_index("dp")
    core = lax.rem(c, 2)
    z = lax.rem(c // 2, n_z)
    y = c // (2 * n_z)
    base = y * (2 * n_z)
    sib = c + 1 - 2 * core
    ypart = (1 - y) * (2 * n_z) + z * 2 + core
    right = base + lax.rem(z + 1, n_z) * 2 + core
    left = base + lax.rem(z + n_z - 1, n_z) * 2 + core
    ring = (right, left)

    def remote(src, dst, s_sem, r_sem, ctx, dp=None):
        return pltpu.make_async_remote_copy(
            src_ref=src,
            dst_ref=dst,
            send_sem=s_sem,
            recv_sem=r_sem,
            device_id=(ctx, g if dp is None else dp),
            device_id_type=MESH,
        )

    def greet(ctx, dp):
        pl.semaphore_signal(
            pltpu.get_barrier_semaphore(), inc=1, device_id=(ctx, dp), device_id_type=MESH
        )

    for other in (sib, ypart, right, left):
        greet(other, g)
    src_core = g // per_core
    src_ctx = c - core + src_core

    def greet_source(i, carry):
        @pl.when(jnp.logical_or(src_ctx != c, i != g))
        def _():
            greet(src_ctx, i)

        return carry

    lax.fori_loop(0, n_dp, greet_source, 0)

    own_q = pl.ds(pl.multiple_of(core * QW, 128), QW)
    sib_q = pl.ds(pl.multiple_of((1 - core) * QW, 128), QW)
    own_k = pl.ds(pl.multiple_of(core * KW, 128), KW)
    sib_k = pl.ds(pl.multiple_of((1 - core) * KW, 128), KW)
    own_rows = pl.ds(pl.multiple_of(core * T, T), T)
    sib_rows = pl.ds(pl.multiple_of((1 - core) * T, T), T)
    copies = [
        pltpu.make_async_copy(pk_in.at[:, own_k], kvb.at[z, 0, 0, own_rows], loc.at[0]),
        pltpu.make_async_copy(pv_in.at[:, own_k], kvb.at[z, 0, 1, own_rows], loc.at[1]),
        pltpu.make_async_copy(q_in.at[:, own_q], raw.at[0, 0], loc.at[2]),
        pltpu.make_async_copy(do_in.at[:, own_q], raw.at[1, 0], loc.at[3]),
        pltpu.make_async_copy(o_in.at[:, own_q], raw.at[2, 0], loc.at[4]),
        pltpu.make_async_copy(kc_in.at[:, own_k], kvc.at[0, pl.ds(0, T)], loc.at[5]),
        pltpu.make_async_copy(vc_in.at[:, own_k], kvc.at[1, pl.ds(0, T)], loc.at[6]),
        pltpu.make_async_copy(st_in, st.at[0], loc.at[7]),
    ]
    for copy in copies:
        copy.start()

    key_at = lax.broadcasted_iota(jnp.int32, (T, 2 * T), 0)
    lane = lax.broadcasted_iota(jnp.int32, (T, 2 * T), 1)
    end0 = len_in[0]
    end1 = end0 + len_in[1]
    end2 = end1 + len_in[2]

    def slot(position):
        return (
            (position >= end0).astype(jnp.int32)
            + (position >= end1).astype(jnp.int32)
            + (position >= end2).astype(jnp.int32)
        )

    def shifted(offset):
        token = lane - offset
        seen = (token >= 0) & (token < T) & (key_at <= token) & (slot(key_at) == slot(token))
        return jnp.where(seen, 0.0, MASKED).astype(BF16)

    bias[0:T, :] = shifted(0)
    bias_own[...] = shifted(T)

    self_target = (src_core == core).astype(jnp.int32)
    pl.semaphore_wait(pltpu.get_barrier_semaphore(), 4 + n_dp - self_target)

    pairs = [
        (pk_in.at[:, sib_k], kvb.at[z, 0, 0, own_rows], kvb.at[z, 0, 0, sib_rows]),
        (pv_in.at[:, sib_k], kvb.at[z, 0, 1, own_rows], kvb.at[z, 0, 1, sib_rows]),
        (q_in.at[:, sib_q], raw.at[0, 1], raw.at[0, 1]),
        (do_in.at[:, sib_q], raw.at[1, 1], raw.at[1, 1]),
        (o_in.at[:, sib_q], raw.at[2, 1], raw.at[2, 1]),
        (kc_in.at[:, sib_k], kvc.at[0, pl.ds(T, T)], kvc.at[0, pl.ds(T, T)]),
        (vc_in.at[:, sib_k], kvc.at[1, pl.ds(T, T)], kvc.at[1, pl.ds(T, T)]),
        (bias_own, bias.at[pl.ds(T, T)], bias.at[pl.ds(T, T)]),
        (st_in, st.at[1], st.at[1]),
    ]
    sends = [
        remote(src, dst, sib_s.at[i], sib_r.at[i], sib) for i, (src, dst, _) in enumerate(pairs)
    ]
    lands = [
        remote(land, land, sib_s.at[i], sib_r.at[i], sib) for i, (_, _, land) in enumerate(pairs)
    ]
    for send in sends:
        send.start()

    def hops(d, r):
        return half - r if d == 0 else half - 1 + r

    def place(d, s):
        return lax.rem(z + (n_z - s if d == 0 else s), n_z)

    def gather_send(buf, s_sem, r_sem, d, r, s):
        block = buf.at[place(d, s), r]
        return remote(block, block, s_sem.at[d, r, s + 1], r_sem.at[d, r, s + 1], ring[d])

    def gather_land(buf, s_sem, r_sem, d, r, s):
        block = buf.at[place(d, s), r]
        return remote(block, block, s_sem.at[d, r, s], r_sem.at[d, r, s], ring[d])

    def gather_start(buf, s_sem, r_sem, slot_y):
        across = remote(buf.at[z, 0], buf.at[z, 1], y_s.at[slot_y], y_r.at[slot_y], ypart)
        across.start()
        for d in (0, 1):
            gather_send(buf, s_sem, r_sem, d, 0, 0).start()
        return across

    def gather_across(buf, s_sem, r_sem, across):
        across.wait_recv()
        for d in (0, 1):
            gather_send(buf, s_sem, r_sem, d, 1, 0).start()

    def gather_step(buf, s_sem, r_sem, s):
        for r in (0, 1):
            for d in (0, 1):

                @pl.when(s <= hops(d, r))
                def _():
                    gather_land(buf, s_sem, r_sem, d, r, s).wait_recv()

                @pl.when(s < hops(d, r))
                def _():
                    gather_send(buf, s_sem, r_sem, d, r, s).start()

    def gather_drain(buf, s_sem, r_sem, across):
        across.wait_send()
        for d in (0, 1):
            for r in (0, 1):

                def drain(s, carry):
                    gather_send(buf, s_sem, r_sem, d, r, s).wait_send()
                    return carry

                lax.fori_loop(0, hops(d, r), drain, 0)

    def spots(s):
        return jnp.where((s == 0) | (s == half), 1, 2)

    for i in (0, 1):
        copies[i].wait()
        lands[i].wait_recv()
    kv_across = gather_start(kvb, kv_s, kv_r, 0)

    for i in (2, 3, 4):
        copies[i].wait()
        lands[i].wait_recv()
    for h in range(HEADS):
        for j in range(GROUP):
            at = (h * GROUP + j) * HEAD_SIZE
            rows = slice(j * BLOCK, (j + 1) * BLOCK)
            q_tile = jnp.concatenate([raw[0, 0, :, at : at + 128], raw[0, 1, :, at : at + 128]], 0)
            do_tile = jnp.concatenate([raw[1, 0, :, at : at + 128], raw[1, 1, :, at : at + 128]], 0)
            o_tile = jnp.concatenate([raw[2, 0, :, at : at + 128], raw[2, 1, :, at : at + 128]], 0)
            qs[h, rows, :] = q_tile
            dos[h, rows, :] = do_tile
            q_t[h, :, rows] = q_tile.T
            do_t[h, :, rows] = do_tile.T
            product = do_tile.astype(F32) * o_tile.astype(F32)
            delta[h, :, rows] = jnp.sum(product.T, axis=0, keepdims=True)

    def merge(h, scores):
        old = top[h]
        new = jnp.maximum(old, jnp.max(scores, axis=0, keepdims=True))
        total[h] = total[h] * jnp.exp2(old - new) + jnp.sum(
            jnp.exp2(scores - new), axis=0, keepdims=True
        )
        top[h] = new

    for i in (5, 6):
        copies[i].wait()
        lands[i].wait_recv()
    lands[7].wait_recv()
    mask_tile = bias[...].astype(F32)
    for h in range(HEADS):
        scores = dot(kvc[0, :, h * 128 : (h + 1) * 128], q_t[h]) * (SCALE * LOG2E)
        scores = scores + jnp.concatenate([mask_tile] * GROUP, axis=1)
        sc[h] = scores
        new = jnp.max(scores, axis=0, keepdims=True)
        top[h] = new
        total[h] = jnp.sum(jnp.exp2(scores - new), axis=0, keepdims=True)
        dq_t[h] = jnp.zeros((HEAD_SIZE, ROWS), F32)

    def first_pass(s):
        def one(i, carry):
            pos = lax.rem(z + n_z + (1 - 2 * i) * s, n_z)
            for h in range(HEADS):
                keys = kvb[pos, :, 0, :, h * 128 : (h + 1) * 128].reshape(2 * BLOCK, HEAD_SIZE)
                scores = dot(keys, q_t[h]) * (SCALE * LOG2E)
                sbuf[h, pos] = scores
                merge(h, scores)
            return carry

        lax.fori_loop(0, spots(s), one, 0)

    gather_across(kvb, kv_s, kv_r, kv_across)

    def kv_slot(s, carry):
        @pl.when(s > 0)
        def _():
            gather_step(kvb, kv_s, kv_r, s)

        first_pass(s)
        return carry

    lax.fori_loop(0, half + 1, kv_slot, 0)
    for h in range(HEADS):
        top[h] = top[h] + jnp.log2(total[h])

    def key_terms(h, scores, keys, values):
        probs = jnp.exp2(scores - top[h])
        dprobs = dot(values, do_t[h])
        dscores = (probs * (dprobs - delta[h])).astype(BF16)
        dv = dot(probs.astype(BF16), dos[h])
        dk = dot(dscores, qs[h]) * SCALE
        dq_t[h] += dot(keys, dscores, 0, 0)
        return dk, dv

    def second_pass(s):
        def one(i, carry):
            pos = lax.rem(z + n_z + (1 - 2 * i) * s, n_z)
            for h in range(HEADS):
                lanes = slice(h * 128, (h + 1) * 128)
                keys = kvb[pos, :, 0, :, lanes].reshape(2 * BLOCK, HEAD_SIZE)
                values = kvb[pos, :, 1, :, lanes].reshape(2 * BLOCK, HEAD_SIZE)
                dk, dv = key_terms(h, sbuf[h, pos], keys, values)
                part[i, :, 0, :, lanes] = dk.reshape(2, BLOCK, HEAD_SIZE)
                part[i, :, 1, :, lanes] = dv.reshape(2, BLOCK, HEAD_SIZE)
            return carry

        lax.fori_loop(0, spots(s), one, 0)

    def sum_send(d, r, s):
        return remote(
            sb.at[d, r, s], rb.at[d, r, s - 1], rs_s.at[d, r, s], rs_r.at[d, r, s - 1], ring[d]
        )

    def sum_land(d, r, s):
        return remote(
            sb.at[d, r, s], rb.at[d, r, s], rs_s.at[d, r, s], rs_r.at[d, r, s], ring[d]
        )

    def sum_slot(u, carry):
        s = half - u
        second_pass(s)
        for d in (0, 1):
            spot = 0 if d == 0 else jnp.where(s == half, 0, 1)
            for r in (0, 1):

                @pl.when(s == hops(d, r))
                def _():
                    sb[d, r, s] = part[spot, r].astype(BF16)

                @pl.when(s < hops(d, r))
                def _():
                    sum_land(d, r, s).wait_recv()
                    sb[d, r, s] = (part[spot, r] + rb[d, r, s].astype(F32)).astype(BF16)

                @pl.when(s <= hops(d, r))
                def _():
                    sum_send(d, r, s).start()

        return carry

    lax.fori_loop(0, half, sum_slot, 0)
    second_pass(0)

    def arrived(r):
        for d in (0, 1):
            sum_land(d, r, 0).wait_recv()
        return part[0, r] + rb[0, r, 0].astype(F32) + rb[1, r, 0].astype(F32)

    yb[0] = arrived(1).astype(BF16)
    cross = remote(yb.at[0], yb.at[1], y_s.at[1], y_r.at[1], ypart)
    cross.start()

    for h in range(HEADS):
        lanes = slice(h * 128, (h + 1) * 128)
        dk, dv = key_terms(h, sc[h], kvc[0, :, lanes], kvc[1, :, lanes])
        gkvc[0, :, lanes] = dk.astype(BF16)
        gkvc[1, :, lanes] = dv.astype(BF16)
        for j in range(GROUP):
            at = (h * GROUP + j) * HEAD_SIZE
            tile = (dq_t[h, :, j * BLOCK : (j + 1) * BLOCK].T * SCALE).astype(BF16)
            gqs[0, :, at : at + 128] = tile[:T]
            gqs[1, :, at : at + 128] = tile[T:]

    def give(i, src_own, src_sib, out, lanes):
        return (
            pltpu.make_async_copy(src_own, out.at[:, lanes], loc.at[i]),
            remote(src_sib, out.at[:, lanes], ret_s.at[i], ret_r.at[i], sib),
        )

    gives = [
        give(0, gqs.at[0], gqs.at[1], gq_out, own_q),
        give(1, gkvc.at[0, pl.ds(0, T)], gkvc.at[0, pl.ds(T, T)], gkc_out, own_k),
        give(2, gkvc.at[1, pl.ds(0, T)], gkvc.at[1, pl.ds(T, T)], gvc_out, own_k),
    ]
    for near, far in gives:
        near.start()
        far.start()

    sum0 = arrived(0)
    cross.wait_recv()
    sum0 = (sum0 + yb[1].astype(F32)).astype(BF16)
    dkb[z, 0] = sum0[0]
    dvf[...] = sum0[1]
    dk_across = gather_start(dkb, dk_s, dk_r, 2)
    late = [
        give(3, dkb.at[z, 0, own_rows], dkb.at[z, 0, sib_rows], gpk_out, own_k),
        give(4, dvf.at[own_rows], dvf.at[sib_rows], gpv_out, own_k),
    ]
    for near, far in late:
        near.start()
        far.start()
    copies[7].wait()
    lands[8].wait_recv()
    proj[...] = jnp.zeros(proj.shape, F32)

    def project(s):
        def one(i, carry):
            pos = lax.rem(z + n_z + (1 - 2 * i) * s, n_z)
            for r in (0, 1):
                row = ((y if r == 0 else 1 - y) * n_z + pos) * BLOCK
                rows = pl.ds(pl.multiple_of(row, BLOCK), BLOCK)
                keys_grad = dkb[pos, r].T
                for i_st in (0, 1):
                    proj[i_st] += dot(keys_grad, st[i_st, rows, :])
            return carry

        lax.fori_loop(0, spots(s), one, 0)

    gather_across(dkb, dk_s, dk_r, dk_across)

    def dk_slot(s, carry):
        @pl.when(s > 0)
        def _():
            gather_step(dkb, dk_s, dk_r, s)

        project(s)
        return carry

    lax.fori_loop(0, half + 1, dk_slot, 0)

    def proj_send(i_st, t):
        rows = pl.ds(pl.multiple_of(t * cols, cols), cols)
        return remote(
            proj.at[i_st, rows],
            prx.at[g],
            pj_s.at[i_st, t],
            pj_r.at[g],
            c if i_st == 0 else sib,
            core * per_core + t,
        )

    def scatter(t, carry):
        @pl.when(core * per_core + t != g)
        def _():
            proj_send(0, t).start()

        @pl.when(core * per_core + t == g)
        def _():
            rows = pl.ds(pl.multiple_of(t * cols, cols), cols)
            prx[g] = proj[0, rows]

        proj_send(1, t).start()
        return carry

    lax.fori_loop(0, per_core, scatter, 0)

    def collect(i, acc):
        @pl.when(jnp.logical_or(src_ctx != c, i != g))
        def _():
            remote(prx.at[i], prx.at[i], pj_s.at[0, 0], pj_r.at[i], sib).wait_recv()

        return acc + prx[i]

    gproj_out[...] = lax.fori_loop(0, n_dp, collect, jnp.zeros(gproj_out.shape, F32))

    def scatter_drain(t, carry):
        @pl.when(core * per_core + t != g)
        def _():
            proj_send(0, t).wait_send()

        proj_send(1, t).wait_send()
        return carry

    lax.fori_loop(0, per_core, scatter_drain, 0)
    for send in sends:
        send.wait_send()
    gather_drain(kvb, kv_s, kv_r, kv_across)
    gather_drain(dkb, dk_s, dk_r, dk_across)
    cross.wait_send()
    for d in (0, 1):
        for r in (0, 1):

            def drain(s, carry):
                sum_send(d, r, s).wait_send()
                return carry

            lax.fori_loop(1, hops(d, r) + 1, drain, 0)
    for near, far in gives + late:
        near.wait()
        far.wait()


def body(q, do, o, kc, vc, pk, pv, states, lengths):
    n_ctx = lax.axis_size("ctx")
    n_dp = lax.axis_size("dp")
    n_z = n_ctx // 4
    half = n_z // 2
    prompt = states.shape[1]
    width = states.shape[2]
    cols = KEY_HEAD_COUNT * HEAD_SIZE // n_dp
    hbm = pl.BlockSpec(memory_space=pl.ANY)
    dma = pltpu.SemaphoreType.DMA
    out = pl.pallas_call(
        functools.partial(kernel, n_z, n_dp),
        out_shape=[
            jax.ShapeDtypeStruct(q.shape[1:], BF16),
            jax.ShapeDtypeStruct(kc.shape[1:], BF16),
            jax.ShapeDtypeStruct(vc.shape[1:], BF16),
            jax.ShapeDtypeStruct(pk.shape[1:], BF16),
            jax.ShapeDtypeStruct(pv.shape[1:], BF16),
            jax.ShapeDtypeStruct((cols, width), F32),
        ],
        in_specs=[hbm] * 8 + [pl.BlockSpec(memory_space=pltpu.SMEM)],
        out_specs=[hbm] * 5 + [pl.BlockSpec(memory_space=pltpu.VMEM)],
        scratch_shapes=[
            pltpu.VMEM((n_z, 2, 2, BLOCK, KW), BF16),
            pltpu.VMEM((3, 2, T, QW), BF16),
            pltpu.VMEM((2, BLOCK, KW), BF16),
            pltpu.VMEM((T, BLOCK), BF16),
            pltpu.VMEM((BLOCK, BLOCK), BF16),
            pltpu.VMEM((2, prompt, width), BF16),
            pltpu.VMEM((HEADS, ROWS, HEAD_SIZE), BF16),
            pltpu.VMEM((HEADS, ROWS, HEAD_SIZE), BF16),
            pltpu.VMEM((HEADS, HEAD_SIZE, ROWS), BF16),
            pltpu.VMEM((HEADS, HEAD_SIZE, ROWS), BF16),
            pltpu.VMEM((HEADS, 1, ROWS), F32),
            pltpu.VMEM((HEADS, 1, ROWS), F32),
            pltpu.VMEM((HEADS, 1, ROWS), F32),
            pltpu.VMEM((HEADS, n_z, 2 * BLOCK, ROWS), F32),
            pltpu.VMEM((HEADS, BLOCK, ROWS), F32),
            pltpu.VMEM((HEADS, HEAD_SIZE, ROWS), F32),
            pltpu.VMEM((2, 2, 2, BLOCK, KW), F32),
            pltpu.VMEM((2, 2, half + 1, 2, BLOCK, KW), BF16),
            pltpu.VMEM((2, 2, half + 1, 2, BLOCK, KW), BF16),
            pltpu.VMEM((2, 2, BLOCK, KW), BF16),
            pltpu.VMEM((n_z, 2, BLOCK, KW), BF16),
            pltpu.VMEM((BLOCK, KW), BF16),
            pltpu.VMEM((2, KW, width), F32),
            pltpu.VMEM((n_dp, cols, width), F32),
            pltpu.VMEM((2, T, QW), BF16),
            pltpu.VMEM((2, BLOCK, KW), BF16),
            dma((8,)),
            dma((9,)),
            dma((9,)),
            dma((3,)),
            dma((3,)),
            dma((2, 2, half + 1)),
            dma((2, 2, half + 1)),
            dma((2, 2, half + 1)),
            dma((2, 2, half + 1)),
            dma((2, 2, half + 1)),
            dma((2, 2, half + 1)),
            dma((2, n_dp // 2)),
            dma((n_dp,)),
            dma((5,)),
            dma((5,)),
        ],
        compiler_params=pltpu.CompilerParams(
            collective_id=0, has_side_effects=True, vmem_limit_bytes=56 * 2**20
        ),
    )(q[0], do[0], o[0], kc[0], vc[0], pk[0], pv[0], states[0], lengths[0, 0])
    return (*(x[None] for x in out[:5]), out[5].T)


def solution(mesh):
    split = P("dp", "ctx", None)
    return jax.shard_map(
        body,
        mesh=mesh,
        in_specs=(split,) * 7 + (P("dp", None, "ctx"), split),
        out_specs=(split,) * 5 + (P("ctx", "dp"),),
        check_vma=False,
    )
```

time: 983 us -> 119 us (0.12); the launches traced: 965 us -> 119 us
  waiting for transfers between devices: 560 us -> 0 us
  starting transfers between devices: 188 us -> 0 us
  Pallas kernels: 0 us -> 110 us
  matrix products: 93.8 us -> 0 us
  local copies, waits for them, and re-layouts: 77.7 us -> 7.91 us
  other arithmetic: 27.9 us -> 0 us
  between operations: 14 us -> 0.66 us
    ppermute x95 -> x0, waiting for transfers between devices: 318 us -> none  [passed_along(): return lax.ppermute(value, axis, pairs)]
    ppermute x95 -> x0, starting transfers between devices: 188 us -> none  [passed_along(): return lax.ppermute(value, axis, pairs)]
    all_gather x2 -> x0, waiting for transfers between devices: 173 us -> none  [the longest x1 90.9 us: body(): all_keys = lax.all_gather(prompt_key_block, 'ctx', axis=0, tiled=True)]
    pallas_call x0 -> x1, Pallas kernels: none -> 110 us  [body(): pl.pallas_call(functools.partial(kernel, n_z, n_dp), out_shape=[jax.Shape...]
    dot_general x170 -> x0, matrix products: 93.8 us -> none  [the longest x33 37.3 us: key_grads(): jnp.einsum('chgd,khd->chgk', cotangent_by_head, heads_of_value, preferred...]
    unnamed x4 -> x0, waiting for transfers between devices: 68.8 us -> none
    dynamic_slice x32 -> x0, local copies, waits for them, and re-layouts: 27.2 us -> none  [keys_at(): lax.dynamic_slice_in_dim(all_keys, shard_of(step_index) * shard_rows, sha...]
    while x31 -> x0, local copies, waits for them, and re-layouts: 26 us -> none
  transfers between devices with their start and end apart: 98 -> 0, of which waited for: 94 -> 0; matrix products, arithmetic and copies ran while one was open for 15% -> 0% of each run, Pallas kernels for 0% -> 0%
where the time goes in v1:
time: 119 us
  Pallas kernels  110 us (92%)
  local copies, waits for them, and re-layouts  7.91 us (7%)
    pallas_call x1, Pallas kernels, body(): pl.pallas_call(functools.partial(kernel, n_z, n_dp), out_shape=[jax.Shape...  110 us
    unnamed x17, local copies, waits for them, and re-layouts  7.91 us

profile of v1, /device:TPU:1, one launch (start us, length us, event | category | flops | bytes accessed | tf_op | source)
XLA Modules:
  0.0 118.8 jit_solution(10578218474066646875)
XLA Ops:
  0.6 2.2 %copy.15 = bf16[1,2048,160]{2,1,0:T(8,128)(2,1)} copy(bf16[1,2048,160]{1,2,0:T(8,128)(2,1)} %param.16) | data formatting | bytes 1310720 | tf_op args[7]
  2.8 110.3 %shard_map.136 = (bf16[64,2560]{1,0:T(8,128)(2,1)}, bf16[64,512]{1,0:T(8,128)(2,1)}, bf16[64,512]{1,0:T(8,128)(2,1)}, bf16[64,512]{1,0:T(8,128)(2,1)}, bf16[64,512]{1,0:T(8,128)(2,1)}, /*index=5*/f32[32,160]{1,0:T(8,128)}) custom-call(bf16[64,2560]{1,0:T(8,128)(2,1)} %bitcast.16, bf16[64,2560]{1,0:T(8,128)(2,1)} %bitcast.17, bf16[64,2560]{1,0:T(8,128)(2,1)} %bitcast.18, ...), custom_call_target="tpu_custom_call" | custom-call | tf_op jit(solution)/shard_map/pallas_call | solution.py:530
  113.1 0.0 copy-start.3
  113.1 1.7 %copy.22 = bf16[1,64,2560]{2,1,0:T(8,128)(2,1)} copy(bf16[1,64,2560]{2,1,0:T(8,128)(2,1)} %bitcast.19) | data formatting | bytes 655360
  114.9 0.0 copy-done.3
  114.9 0.0 copy-start.2
  114.9 0.6 copy.23
  115.5 0.2 copy-done.2
  115.7 0.0 copy-start.1
  115.7 0.6 copy.24
  116.4 0.2 copy-done.1
  116.6 0.0 copy-start
  116.6 0.6 copy.25
  117.2 0.2 copy-done
  117.5 0.0 copy-start.4
  117.5 0.6 copy.26
  118.1 0.1 copy-done.4
  118.2 0.6 copy.27
Async XLA Ops:
  113.1 1.8 %copy-start.3 = (bf16[64,512]{1,0:T(8,128)(2,1)S(1)}, bf16[64,512]{1,0:T(8,128)(2,1)}, u32[]{:S(2)}) copy-start(bf16[64,512]{1,0:T(8,128)(2,1)} %get-tuple-element.13) | copy-start | bytes 196612
  114.9 0.9 copy-start.2
  115.7 0.9 copy-start.1
  116.6 0.9 copy-start
  117.5 0.8 copy-start.4

commit v2 on v1

v2 whole, which is shorter than its diff:
```python
import functools
import math

import jax
import jax.numpy as jnp
from jax import lax
from jax.experimental import pallas as pl
from jax.experimental.pallas import tpu as pltpu
from jax.sharding import PartitionSpec as P

QUERY_HEAD_COUNT = 20
KEY_HEAD_COUNT = 4
HEAD_SIZE = 128
GROUP = QUERY_HEAD_COUNT // KEY_HEAD_COUNT
MASKED = -1e30
SCALE = HEAD_SIZE ** (-0.5)
LOG2E = math.log2(math.e)
MESH = pl.DeviceIdType.MESH
F32 = jnp.float32
BF16 = jnp.bfloat16

HEADS = KEY_HEAD_COUNT // 2
KW = HEADS * HEAD_SIZE
QW = HEADS * GROUP * HEAD_SIZE
T = 64
ROWS = GROUP * 2 * T
BLOCK = 2 * T


def dot(a, b, ca=1, cb=0):
    return lax.dot_general(a, b, (((ca,), (cb,)), ((), ())), preferred_element_type=F32)


def kernel(
    n_z,
    n_dp,
    q_in,
    do_in,
    o_in,
    kc_in,
    vc_in,
    pk_in,
    pv_in,
    st_in,
    len_in,
    gq_out,
    gkc_out,
    gvc_out,
    gpk_out,
    gpv_out,
    gproj_out,
    kb,
    vb,
    raw,
    kvc,
    bias_own,
    bias,
    st,
    qs,
    dos,
    q_t,
    do_t,
    delta,
    top,
    total,
    sbuf,
    sc,
    dq_t,
    part,
    sb,
    rb,
    yb,
    dkb,
    dvf,
    proj,
    pack,
    prx,
    gqs,
    gkvc,
    loc,
    sib_s,
    sib_r,
    y_s,
    y_r,
    k_s,
    k_r,
    v_s,
    v_r,
    rs_s,
    rs_r,
    dk_s,
    dk_r,
    pj_s,
    pj_r,
    ret_s,
    ret_r,
):
    half = n_z // 2
    per_core = n_dp // 2
    cols = KEY_HEAD_COUNT * HEAD_SIZE // n_dp
    width = st.shape[1]
    c = lax.axis_index("ctx")
    g = lax.axis_index("dp")
    core = lax.rem(c, 2)
    z = lax.rem(c // 2, n_z)
    y = c // (2 * n_z)
    base = y * (2 * n_z)
    sib = c + 1 - 2 * core
    ypart = (1 - y) * (2 * n_z) + z * 2 + core
    right = base + lax.rem(z + 1, n_z) * 2 + core
    left = base + lax.rem(z + n_z - 1, n_z) * 2 + core
    ring = (right, left)

    def remote(src, dst, s_sem, r_sem, ctx, dp=None):
        return pltpu.make_async_remote_copy(
            src_ref=src,
            dst_ref=dst,
            send_sem=s_sem,
            recv_sem=r_sem,
            device_id=(ctx, g if dp is None else dp),
            device_id_type=MESH,
        )

    def greet(ctx, dp):
        pl.semaphore_signal(
            pltpu.get_barrier_semaphore(), inc=1, device_id=(ctx, dp), device_id_type=MESH
        )

    for other in (sib, ypart, right, left):
        greet(other, g)
    src_core = g // per_core
    src_ctx = c - core + src_core

    def greet_source(i, carry):
        @pl.when(jnp.logical_or(src_ctx != c, i != g))
        def _():
            greet(src_ctx, i)

        return carry

    lax.fori_loop(0, n_dp, greet_source, 0)

    own_q = pl.ds(pl.multiple_of(core * QW, 128), QW)
    sib_q = pl.ds(pl.multiple_of((1 - core) * QW, 128), QW)
    own_k = pl.ds(pl.multiple_of(core * KW, 128), KW)
    sib_k = pl.ds(pl.multiple_of((1 - core) * KW, 128), KW)
    own_rows = pl.ds(pl.multiple_of(core * T, T), T)
    sib_rows = pl.ds(pl.multiple_of((1 - core) * T, T), T)
    def head_lanes(which, h):
        return pl.ds(pl.multiple_of(which * KW + h * HEAD_SIZE, 128), HEAD_SIZE)

    copies = [
        pltpu.make_async_copy(source.at[:, head_lanes(core, h)], buf.at[z, 0, h, own_rows], loc.at[i])
        for i, (source, buf, h) in enumerate(
            [(pk_in, kb, 0), (pk_in, kb, 1), (pv_in, vb, 0), (pv_in, vb, 1)]
        )
    ] + [
        pltpu.make_async_copy(q_in.at[:, own_q], raw.at[0, 0], loc.at[4]),
        pltpu.make_async_copy(do_in.at[:, own_q], raw.at[1, 0], loc.at[5]),
        pltpu.make_async_copy(o_in.at[:, own_q], raw.at[2, 0], loc.at[6]),
        pltpu.make_async_copy(kc_in.at[:, own_k], kvc.at[0, pl.ds(0, T)], loc.at[7]),
        pltpu.make_async_copy(vc_in.at[:, own_k], kvc.at[1, pl.ds(0, T)], loc.at[8]),
        pltpu.make_async_copy(st_in, st.at[0], loc.at[9]),
    ]
    for copy in copies:
        copy.start()

    key_at = lax.broadcasted_iota(jnp.int32, (T, 2 * T), 0)
    lane = lax.broadcasted_iota(jnp.int32, (T, 2 * T), 1)
    end0 = len_in[0]
    end1 = end0 + len_in[1]
    end2 = end1 + len_in[2]

    def slot(position):
        return (
            (position >= end0).astype(jnp.int32)
            + (position >= end1).astype(jnp.int32)
            + (position >= end2).astype(jnp.int32)
        )

    def shifted(offset):
        token = lane - offset
        seen = (token >= 0) & (token < T) & (key_at <= token) & (slot(key_at) == slot(token))
        return jnp.where(seen, 0.0, MASKED).astype(BF16)

    bias[0:T, :] = shifted(0)
    bias_own[...] = shifted(T)

    self_target = (src_core == core).astype(jnp.int32)
    pl.semaphore_wait(pltpu.get_barrier_semaphore(), 4 + n_dp - self_target)

    pairs = [
        (source.at[:, head_lanes(1 - core, h)], buf.at[z, 0, h, own_rows], buf.at[z, 0, h, sib_rows])
        for source, buf, h in [(pk_in, kb, 0), (pk_in, kb, 1), (pv_in, vb, 0), (pv_in, vb, 1)]
    ] + [
        (q_in.at[:, sib_q], raw.at[0, 1], raw.at[0, 1]),
        (do_in.at[:, sib_q], raw.at[1, 1], raw.at[1, 1]),
        (o_in.at[:, sib_q], raw.at[2, 1], raw.at[2, 1]),
        (kc_in.at[:, sib_k], kvc.at[0, pl.ds(T, T)], kvc.at[0, pl.ds(T, T)]),
        (vc_in.at[:, sib_k], kvc.at[1, pl.ds(T, T)], kvc.at[1, pl.ds(T, T)]),
        (st_in, st.at[1], st.at[1]),
        (bias_own, bias.at[pl.ds(T, T)], bias.at[pl.ds(T, T)]),
    ]
    sends = [
        remote(src, dst, sib_s.at[i], sib_r.at[i], sib) for i, (src, dst, _) in enumerate(pairs)
    ]
    lands = [
        remote(land, land, sib_s.at[i], sib_r.at[i], sib) for i, (_, _, land) in enumerate(pairs)
    ]
    for i in (0, 1, 2, 3, 4, 5, 6, 7, 8, 10, 9):
        sends[i].start()

    def hops(d, r):
        return half - r if d == 0 else half - 1 + r

    def place(d, s):
        return lax.rem(z + (n_z - s if d == 0 else s), n_z)

    def gather_send(buf, s_sem, r_sem, d, r, h, s):
        block = buf.at[place(d, s), r, h]
        return remote(block, block, s_sem.at[d, r, h, s + 1], r_sem.at[d, r, h, s + 1], ring[d])

    def gather_land(buf, s_sem, r_sem, d, r, h, s):
        block = buf.at[place(d, s), r, h]
        return remote(block, block, s_sem.at[d, r, h, s], r_sem.at[d, r, h, s], ring[d])

    def gather_start(buf, s_sem, r_sem, r, h):
        for d in (0, 1):
            gather_send(buf, s_sem, r_sem, d, r, h, 0).start()

    def across(src, dst, i):
        return remote(src, dst, y_s.at[i], y_r.at[i], ypart)

    def gather_step(buf, s_sem, r_sem, s, heads):
        for r in (0, 1):
            for h in heads:
                for d in (0, 1):

                    @pl.when(s <= hops(d, r))
                    def _():
                        gather_land(buf, s_sem, r_sem, d, r, h, s).wait_recv()

                    @pl.when(s < hops(d, r))
                    def _():
                        gather_send(buf, s_sem, r_sem, d, r, h, s).start()

    def gather_drain(buf, s_sem, r_sem):
        for d in (0, 1):
            for r in (0, 1):

                def drain(s, carry):
                    for h in range(HEADS):
                        gather_send(buf, s_sem, r_sem, d, r, h, s).wait_send()
                    return carry

                lax.fori_loop(0, hops(d, r), drain, 0)

    def spots(s):
        return jnp.where((s == 0) | (s == half), 1, 2)

    def landed(*which):
        for i in which:
            copies[i].wait()
            lands[i].wait_recv()

    keys, values = (kb, k_s, k_r), (vb, v_s, v_r)
    crossings = []
    for kind, chain in enumerate((keys, values)):
        for h in range(HEADS):
            landed(2 * kind + h)
            gather_start(*chain, 0, h)
            crossings.append(across(chain[0].at[z, 0, h], chain[0].at[z, 1, h], 2 * kind + h))
            crossings[-1].start()

    def tiles(i, h, j):
        at = (h * GROUP + j) * HEAD_SIZE
        return jnp.concatenate([raw[i, 0, :, at : at + 128], raw[i, 1, :, at : at + 128]], 0)

    landed(4)
    for h in range(HEADS):
        for j in range(GROUP):
            rows = slice(j * BLOCK, (j + 1) * BLOCK)
            q_tile = tiles(0, h, j)
            qs[h, rows, :] = q_tile
            q_t[h, :, rows] = q_tile.T

    def merge(h, scores):
        old = top[h]
        new = jnp.maximum(old, jnp.max(scores, axis=0, keepdims=True))
        total[h] = total[h] * jnp.exp2(old - new) + jnp.sum(
            jnp.exp2(scores - new), axis=0, keepdims=True
        )
        top[h] = new

    for h in range(HEADS):
        crossings[h].wait_recv()
        gather_start(*keys, 1, h)
    landed(7, 8)
    lands[10].wait_recv()
    mask_tile = bias[...].astype(F32)
    for h in range(HEADS):
        scores = dot(kvc[0, :, h * 128 : (h + 1) * 128], q_t[h]) * (SCALE * LOG2E)
        scores = scores + jnp.concatenate([mask_tile] * GROUP, axis=1)
        sc[h] = scores
        new = jnp.max(scores, axis=0, keepdims=True)
        top[h] = new
        total[h] = jnp.sum(jnp.exp2(scores - new), axis=0, keepdims=True)
        dq_t[h] = jnp.zeros((HEAD_SIZE, ROWS), F32)

    def first_pass(s):
        def one(i, carry):
            pos = lax.rem(z + n_z + (1 - 2 * i) * s, n_z)
            for h in range(HEADS):
                block = kb[pos, :, h].reshape(2 * BLOCK, HEAD_SIZE)
                scores = dot(block, q_t[h]) * (SCALE * LOG2E)
                sbuf[h, pos] = scores
                merge(h, scores)
            return carry

        lax.fori_loop(0, spots(s), one, 0)

    first_pass(0)
    for h in range(HEADS):
        crossings[2 + h].wait_recv()
        gather_start(*values, 1, h)
    landed(5, 6)
    for h in range(HEADS):
        for j in range(GROUP):
            rows = slice(j * BLOCK, (j + 1) * BLOCK)
            do_tile = tiles(1, h, j)
            dos[h, rows, :] = do_tile
            do_t[h, :, rows] = do_tile.T
            product = do_tile.astype(F32) * tiles(2, h, j).astype(F32)
            delta[h, :, rows] = jnp.sum(product.T, axis=0, keepdims=True)

    def gather_slot(s, carry):
        gather_step(*keys, s, range(HEADS))
        gather_step(*values, s, range(HEADS))
        first_pass(s)
        return carry

    lax.fori_loop(1, half + 1, gather_slot, 0)
    for h in range(HEADS):
        top[h] = top[h] + jnp.log2(total[h])

    def key_terms(h, scores, key_block, value_block):
        probs = jnp.exp2(scores - top[h])
        dprobs = dot(value_block, do_t[h])
        dscores = (probs * (dprobs - delta[h])).astype(BF16)
        dv = dot(probs.astype(BF16), dos[h])
        dk = dot(dscores, qs[h]) * SCALE
        dq_t[h] += dot(key_block, dscores, 0, 0)
        return dk, dv

    def second_pass(s):
        def one(i, carry):
            pos = lax.rem(z + n_z + (1 - 2 * i) * s, n_z)
            for h in range(HEADS):
                key_block = kb[pos, :, h].reshape(2 * BLOCK, HEAD_SIZE)
                value_block = vb[pos, :, h].reshape(2 * BLOCK, HEAD_SIZE)
                dk, dv = key_terms(h, sbuf[h, pos], key_block, value_block)
                part[0, pos, :, h] = dk.reshape(2, BLOCK, HEAD_SIZE)
                part[1, pos, :, h] = dv.reshape(2, BLOCK, HEAD_SIZE)
            return carry

        lax.fori_loop(0, spots(s), one, 0)

    def sum_send(kind, d, r, h, s):
        return remote(
            sb.at[kind, d, r, h, s],
            rb.at[kind, d, r, h, s - 1],
            rs_s.at[kind, d, r, h, s],
            rs_r.at[kind, d, r, h, s - 1],
            ring[d],
        )

    def sum_land(kind, d, r, h, s):
        block = rb.at[kind, d, r, h, s]
        return remote(block, block, rs_s.at[kind, d, r, h, s], rs_r.at[kind, d, r, h, s], ring[d])

    def own_term(kind, d, r, h, s):
        return part[kind, place(1 - d, s), r, h]

    def sum_step(kind, s):
        for r in (1, 0):
            for h in range(HEADS):
                for d in (0, 1):

                    @pl.when(s == hops(d, r))
                    def _():
                        sb[kind, d, r, h, s] = own_term(kind, d, r, h, s).astype(BF16)

                    @pl.when(s < hops(d, r))
                    def _():
                        sum_land(kind, d, r, h, s).wait_recv()
                        sb[kind, d, r, h, s] = (
                            own_term(kind, d, r, h, s) + rb[kind, d, r, h, s].astype(F32)
                        ).astype(BF16)

                    @pl.when(s <= hops(d, r))
                    def _():
                        sum_send(kind, d, r, h, s).start()

    def arrived(kind, r, h):
        for d in (0, 1):
            sum_land(kind, d, r, h, 0).wait_recv()
        return (
            part[kind, z, r, h] + rb[kind, 0, r, h, 0].astype(F32) + rb[kind, 1, r, h, 0].astype(F32)
        )

    def sum_slot(u, carry):
        s = half - u
        second_pass(s)
        sum_step(0, s)
        return carry

    lax.fori_loop(0, half, sum_slot, 0)
    second_pass(0)

    def swap(kind, r, h):
        yb[kind, r, h, 0] = arrived(kind, r, h).astype(BF16)
        i = 4 + (kind * 2 + r) * HEADS + h
        crossing = across(yb.at[kind, r, h, 0], yb.at[kind, 1 - r, h, 1], i)
        crossing.start()
        return crossing, across(yb.at[kind, r, h, 1], yb.at[kind, r, h, 1], 4 + (kind * 2 + 1 - r) * HEADS + h)

    swaps = {}
    for h in range(HEADS):
        for r in (1, 0):
            swaps[0, r, h] = swap(0, r, h)
    sum_step(1, half)

    for h in range(HEADS):
        lanes = slice(h * 128, (h + 1) * 128)
        dk, dv = key_terms(h, sc[h], kvc[0, :, lanes], kvc[1, :, lanes])
        gkvc[0, :, lanes] = dk.astype(BF16)
        gkvc[1, :, lanes] = dv.astype(BF16)

    for h in range(HEADS):
        for j in range(GROUP):
            at = (h * GROUP + j) * HEAD_SIZE
            tile = (dq_t[h, :, j * BLOCK : (j + 1) * BLOCK].T * SCALE).astype(BF16)
            gqs[0, :, at : at + 128] = tile[:T]
            gqs[1, :, at : at + 128] = tile[T:]

    def give(i, src_own, src_sib, out, lanes):
        return (
            pltpu.make_async_copy(src_own, out.at[:, lanes], loc.at[i]),
            remote(src_sib, out.at[:, lanes], ret_s.at[i], ret_r.at[i], sib),
        )

    gives = [
        give(0, gqs.at[0], gqs.at[1], gq_out, own_q),
        give(1, gkvc.at[0, pl.ds(0, T)], gkvc.at[0, pl.ds(T, T)], gkc_out, own_k),
        give(2, gkvc.at[1, pl.ds(0, T)], gkvc.at[1, pl.ds(T, T)], gvc_out, own_k),
    ]
    for near, far in gives:
        near.start()
        far.start()

    sum_step(1, half - 1)
    copies[9].wait()
    lands[9].wait_recv()
    proj[...] = jnp.zeros(proj.shape, F32)
    grads = (dkb, dk_s, dk_r)

    def finish(kind, r, h):
        swaps[kind, r, h][1].wait_recv()
        near_sum = part[kind, z, r, h] + rb[kind, 0, r, h, 0].astype(F32)
        near_sum = near_sum + rb[kind, 1, r, h, 0].astype(F32)
        return (near_sum + yb[kind, r, h, 1].astype(F32)).astype(BF16)

    def give_prompt(i, buf, out, h):
        lanes = head_lanes(core, h)
        gives.append(give(i, buf.at[own_rows], buf.at[sib_rows], out, lanes))
        for copy in gives[-1]:
            copy.start()

    for r in (0, 1):
        for h in range(HEADS):
            dkb[z, r, h] = finish(0, r, h)
            gather_start(*grads, r, h)
            if r == 0:
                give_prompt(3 + h, dkb.at[z, 0, h], gpk_out, h)

    def project(h, s):
        def one(i, carry):
            pos = lax.rem(z + n_z + (1 - 2 * i) * s, n_z)
            for r in (0, 1):
                row = ((y if r == 0 else 1 - y) * n_z + pos) * BLOCK
                rows = pl.ds(pl.multiple_of(row, BLOCK), BLOCK)
                states = st[:, :, rows].reshape(2 * width, BLOCK)
                proj[h] += dot(states, dkb[pos, r, h])
            return carry

        lax.fori_loop(0, spots(s), one, 0)

    def proj_send(i_st, t):
        return remote(
            pack.at[i_st, t],
            prx.at[g],
            pj_s.at[i_st, t],
            pj_r.at[g],
            c if i_st == 0 else sib,
            core * per_core + t,
        )

    quarter = cols // 4
    lanes_at = lax.broadcasted_iota(jnp.int32, (quarter, HEAD_SIZE), 1) // 32
    per_head = per_core // HEADS

    def scatter(h):
        for i_st in (0, 1):
            turned = proj[h, i_st * width : (i_st + 1) * width].T
            head = turned[:, :128]
            tail = jnp.concatenate([turned[:, 128:], jnp.zeros((HEAD_SIZE, 96), F32)], axis=1)
            for k in range(per_head):
                t = h * per_head + k
                pack[i_st, t, :cols] = head[k * cols : (k + 1) * cols]
                folded = jnp.zeros((quarter, 128), F32)
                for j in range(4):
                    at = k * cols + j * quarter
                    piece = tail[at : at + quarter]
                    if j:
                        piece = pltpu.roll(piece, 32 * j, 1)
                    folded = jnp.where(lanes_at == j, piece, folded)
                pack[i_st, t, cols:] = folded

                @pl.when(core * per_core + t + i_st * n_dp != g)
                def _():
                    proj_send(i_st, t).start()

    for h in range(HEADS):
        project(h, 0)
    for s in range(1, half):
        for h in range(HEADS):
            gather_step(*grads, s, (h,))
        for h in range(HEADS):
            project(h, s)
    for h in range(HEADS):
        gather_step(*grads, half, (h,))
        project(h, half)
        scatter(h)

    @pl.when(src_core == core)
    def _():
        prx[g] = pack[0, g - core * per_core]

    for s in range(half - 2, 0, -1):
        sum_step(1, s)
    for h in range(HEADS):
        yb[1, 1, h, 0] = arrived(1, 1, h).astype(BF16)
        i = 4 + 3 * HEADS + h
        crossing = across(yb.at[1, 1, h, 0], yb.at[1, 0, h, 1], i)
        crossing.start()
        swaps[1, 0, h] = (crossing, across(yb.at[1, 0, h, 1], yb.at[1, 0, h, 1], i))

    def collect(i, acc):
        @pl.when(jnp.logical_or(src_ctx != c, i != g))
        def _():
            remote(prx.at[i], prx.at[i], pj_s.at[0, 0], pj_r.at[i], sib).wait_recv()

        return acc + prx[i]

    summed = lax.fori_loop(0, n_dp, collect, jnp.zeros(prx.shape[1:], F32))
    gproj_out[:, :128] = summed[:cols]
    for j in range(4):
        piece = summed[cols:]
        if j:
            piece = pltpu.roll(piece, 128 - 32 * j, 1)
        gproj_out[j * quarter : (j + 1) * quarter, 128:] = piece[:, :32]

    for h in range(HEADS):
        arrived(1, 0, h)
        dvf[h] = finish(1, 0, h)
        give_prompt(3 + HEADS + h, dvf.at[h], gpv_out, h)

    def scatter_drain(t, carry):
        @pl.when(core * per_core + t != g)
        def _():
            proj_send(0, t).wait_send()

        proj_send(1, t).wait_send()
        return carry

    lax.fori_loop(0, per_core, scatter_drain, 0)
    for send in sends:
        send.wait_send()
    for chain in (keys, values, grads):
        gather_drain(*chain)
    for crossing in crossings:
        crossing.wait_send()
    for crossing, _ in swaps.values():
        crossing.wait_send()
    for kind in (0, 1):
        for d in (0, 1):
            for r in (0, 1):

                def drain(s, carry):
                    for h in range(HEADS):
                        sum_send(kind, d, r, h, s).wait_send()
                    return carry

                lax.fori_loop(1, hops(d, r) + 1, drain, 0)
    for near, far in gives:
        near.wait()
        far.wait()


def hand_on(*refs):
    count = len(refs) // 2
    for source, target in zip(refs[:count], refs[count:]):
        target[...] = source[...]


def body(q, do, o, kc, vc, pk, pv, states, lengths):
    n_ctx = lax.axis_size("ctx")
    n_dp = lax.axis_size("dp")
    n_z = n_ctx // 4
    half = n_z // 2
    prompt = states.shape[1]
    width = states.shape[2]
    cols = KEY_HEAD_COUNT * HEAD_SIZE // n_dp
    hbm = pl.BlockSpec(memory_space=pl.ANY)
    dma = pltpu.SemaphoreType.DMA
    out = pl.pallas_call(
        functools.partial(kernel, n_z, n_dp),
        out_shape=[
            jax.ShapeDtypeStruct(q.shape[1:], BF16),
            jax.ShapeDtypeStruct(kc.shape[1:], BF16),
            jax.ShapeDtypeStruct(vc.shape[1:], BF16),
            jax.ShapeDtypeStruct(pk.shape[1:], BF16),
            jax.ShapeDtypeStruct(pv.shape[1:], BF16),
            jax.ShapeDtypeStruct((cols, width), F32),
        ],
        in_specs=[hbm] * 8 + [pl.BlockSpec(memory_space=pltpu.SMEM)],
        out_specs=[hbm] * 5 + [pl.BlockSpec(memory_space=pltpu.VMEM)],
        scratch_shapes=[
            pltpu.VMEM((n_z, 2, HEADS, BLOCK, HEAD_SIZE), BF16),
            pltpu.VMEM((n_z, 2, HEADS, BLOCK, HEAD_SIZE), BF16),
            pltpu.VMEM((3, 2, T, QW), BF16),
            pltpu.VMEM((2, BLOCK, KW), BF16),
            pltpu.VMEM((T, BLOCK), BF16),
            pltpu.VMEM((BLOCK, BLOCK), BF16),
            pltpu.VMEM((2, width, prompt), BF16),
            pltpu.VMEM((HEADS, ROWS, HEAD_SIZE), BF16),
            pltpu.VMEM((HEADS, ROWS, HEAD_SIZE), BF16),
            pltpu.VMEM((HEADS, HEAD_SIZE, ROWS), BF16),
            pltpu.VMEM((HEADS, HEAD_SIZE, ROWS), BF16),
            pltpu.VMEM((HEADS, 1, ROWS), F32),
            pltpu.VMEM((HEADS, 1, ROWS), F32),
            pltpu.VMEM((HEADS, 1, ROWS), F32),
            pltpu.VMEM((HEADS, n_z, 2 * BLOCK, ROWS), F32),
            pltpu.VMEM((HEADS, BLOCK, ROWS), F32),
            pltpu.VMEM((HEADS, HEAD_SIZE, ROWS), F32),
            pltpu.VMEM((2, n_z, 2, HEADS, BLOCK, HEAD_SIZE), F32),
            pltpu.VMEM((2, 2, 2, HEADS, half + 1, BLOCK, HEAD_SIZE), BF16),
            pltpu.VMEM((2, 2, 2, HEADS, half + 1, BLOCK, HEAD_SIZE), BF16),
            pltpu.VMEM((2, 2, HEADS, 2, BLOCK, HEAD_SIZE), BF16),
            pltpu.VMEM((n_z, 2, HEADS, BLOCK, HEAD_SIZE), BF16),
            pltpu.VMEM((HEADS, BLOCK, HEAD_SIZE), BF16),
            pltpu.VMEM((HEADS, 2 * width, HEAD_SIZE), F32),
            pltpu.VMEM((2, n_dp // 2, cols + cols // 4, 128), F32),
            pltpu.VMEM((n_dp, cols + cols // 4, 128), F32),
            pltpu.VMEM((2, T, QW), BF16),
            pltpu.VMEM((2, BLOCK, KW), BF16),
            dma((10,)),
            dma((11,)),
            dma((11,)),
            dma((12,)),
            dma((12,)),
            *[dma((2, 2, HEADS, half + 1))] * 4,
            dma((2, 2, 2, HEADS, half + 1)),
            dma((2, 2, 2, HEADS, half + 1)),
            *[dma((2, 2, HEADS, half + 1))] * 2,
            dma((2, n_dp // 2)),
            dma((n_dp,)),
            dma((7,)),
            dma((7,)),
        ],
        compiler_params=pltpu.CompilerParams(
            collective_id=0, has_side_effects=True, vmem_limit_bytes=56 * 2**20
        ),
    )(q[0], do[0], o[0], kc[0], vc[0], pk[0], pv[0], states[0].T, lengths[0, 0])
    out = pl.pallas_call(
        hand_on,
        out_shape=[jax.ShapeDtypeStruct(x.shape, x.dtype) for x in out],
    )(*out)
    return (*(x[None] for x in out[:5]), out[5].T)


def solution(mesh):
    split = P("dp", "ctx", None)
    return jax.shard_map(
        body,
        mesh=mesh,
        in_specs=(split,) * 7 + (P("dp", None, "ctx"), split),
        out_specs=(split,) * 5 + (P("ctx", "dp"),),
        check_vma=False,
    )
```

time: 119 us -> 103 us (0.87)
  Pallas kernels: 110 us -> 102 us
  local copies, waits for them, and re-layouts: 7.91 us -> 0 us
    pallas_call x1, Pallas kernels: 110 us -> 99.8 us  [body(): pl.pallas_call(functools.partial(kernel, n_z, n_dp), out_shape=[jax.Shape...]
    unnamed x17 -> x0, local copies, waits for them, and re-layouts: 7.91 us -> none
    pallas_call x0 -> x1, Pallas kernels: none -> 1.87 us  [body(): pl.pallas_call(hand_on, out_shape=[jax.ShapeDtypeStruct(x.shape, x.dtype)...]
where the time goes in v2:
time: 103 us; the launch traced here: 102 us
  Pallas kernels  102 us (99%)
    pallas_call x1, Pallas kernels, body(): pl.pallas_call(functools.partial(kernel, n_z, n_dp), out_shape=[jax.Shape...  99.8 us

profile of v2, /device:TPU:1, one launch (start us, length us, event | category | flops | bytes accessed | tf_op | source)
XLA Modules:
  0.0 102.3 jit_solution(16826818163151428756)
XLA Ops:
  0.6 99.8 %shard_map.136 = (bf16[64,2560]{1,0:T(8,128)(2,1)}, bf16[64,512]{1,0:T(8,128)(2,1)}, bf16[64,512]{1,0:T(8,128)(2,1)}, bf16[64,512]{1,0:T(8,128)(2,1)}, bf16[64,512]{1,0:T(8,128)(2,1)}, /*index=5*/f32[32,160]{1,0:T(8,128)}) custom-call(bf16[64,2560]{1,0:T(8,128)(2,1)} %bitcast.18, bf16[64,2560]{1,0:T(8,128)(2,1)} %bitcast.19, bf16[64,2560]{1,0:T(8,128)(2,1)} %bitcast.20, ...), custom_call_target="tpu_custom_call" | custom-call | tf_op jit(solution)/shard_map/pallas_call | solution.py:626
  100.4 1.9 %shard_map.137 = (bf16[64,2560]{1,0:T(8,128)(2,1)}, bf16[64,512]{1,0:T(8,128)(2,1)}, bf16[64,512]{1,0:T(8,128)(2,1)}, bf16[64,512]{1,0:T(8,128)(2,1)}, bf16[64,512]{1,0:T(8,128)(2,1)}, /*index=5*/f32[32,160]{1,0:T(8,128)}) custom-call(bf16[64,2560]{1,0:T(8,128)(2,1)} %get-tuple-element.18.refs_0_, bf16[64,512]{1,0:T(8,128)(2,1)} %get-tuple-element.19.refs_1_, ...), custom_call_target="tpu_custom_call" | custom-call | tf_op jit(solution)/shard_map/pallas_call | solution.py:685

commit v3 on v2

--- a/solution.py
+++ b/solution.py
@@ -207,7 +207,7 @@
     lands = [
         remote(land, land, sib_s.at[i], sib_r.at[i], sib) for i, (_, _, land) in enumerate(pairs)
     ]
-    for i in (0, 1, 2, 3, 4, 5, 6, 7, 8, 10, 9):
+    for i in range(4):
         sends[i].start()
 
     def hops(d, r):
@@ -231,18 +231,17 @@
     def across(src, dst, i):
         return remote(src, dst, y_s.at[i], y_r.at[i], ypart)
 
-    def gather_step(buf, s_sem, r_sem, s, heads):
-        for r in (0, 1):
-            for h in heads:
-                for d in (0, 1):
-
-                    @pl.when(s <= hops(d, r))
-                    def _():
-                        gather_land(buf, s_sem, r_sem, d, r, h, s).wait_recv()
-
-                    @pl.when(s < hops(d, r))
-                    def _():
-                        gather_send(buf, s_sem, r_sem, d, r, h, s).start()
+    def gather_step(buf, s_sem, r_sem, r, s, heads=range(HEADS)):
+        for h in heads:
+            for d in (0, 1):
+
+                @pl.when((s >= 1) & (s <= hops(d, r)))
+                def _():
+                    gather_land(buf, s_sem, r_sem, d, r, h, s).wait_recv()
+
+                @pl.when((s >= 1) & (s < hops(d, r)))
+                def _():
+                    gather_send(buf, s_sem, r_sem, d, r, h, s).start()
 
     def gather_drain(buf, s_sem, r_sem):
         for d in (0, 1):
@@ -264,13 +263,21 @@
             lands[i].wait_recv()
 
     keys, values = (kb, k_s, k_r), (vb, v_s, v_r)
-    crossings = []
-    for kind, chain in enumerate((keys, values)):
-        for h in range(HEADS):
-            landed(2 * kind + h)
-            gather_start(*chain, 0, h)
-            crossings.append(across(chain[0].at[z, 0, h], chain[0].at[z, 1, h], 2 * kind + h))
-            crossings[-1].start()
+    crossings = [
+        across(buf.at[z, 0, h], buf.at[z, 1, h], 2 * kind + h)
+        for kind, buf in enumerate((kb, vb))
+        for h in range(HEADS)
+    ]
+    for h in range(HEADS):
+        landed(h)
+        gather_start(*keys, 0, h)
+        crossings[h].start()
+    for i in (4, 7, 8, 10, 5, 6, 9):
+        sends[i].start()
+    for h in range(HEADS):
+        landed(2 + h)
+        crossings[2 + h].start()
+        gather_start(*values, 0, h)
 
     def tiles(i, h, j):
         at = (h * GROUP + j) * HEAD_SIZE
@@ -292,9 +299,6 @@
         )
         top[h] = new
 
-    for h in range(HEADS):
-        crossings[h].wait_recv()
-        gather_start(*keys, 1, h)
     landed(7, 8)
     lands[10].wait_recv()
     mask_tile = bias[...].astype(F32)
@@ -319,10 +323,6 @@
 
         lax.fori_loop(0, spots(s), one, 0)
 
-    first_pass(0)
-    for h in range(HEADS):
-        crossings[2 + h].wait_recv()
-        gather_start(*values, 1, h)
     landed(5, 6)
     for h in range(HEADS):
         for j in range(GROUP):
@@ -333,13 +333,26 @@
             product = do_tile.astype(F32) * tiles(2, h, j).astype(F32)
             delta[h, :, rows] = jnp.sum(product.T, axis=0, keepdims=True)
 
-    def gather_slot(s, carry):
-        gather_step(*keys, s, range(HEADS))
-        gather_step(*values, s, range(HEADS))
-        first_pass(s)
+    def gather_slot(i, carry):
+        gather_step(*keys, 0, i)
+        gather_step(*values, 0, i)
+        for lag, chain in ((1, keys), (2, values)):
+
+            @pl.when(i == lag)
+            def _():
+                for h in range(HEADS):
+                    crossings[2 * lag - 2 + h].wait_recv()
+                    gather_start(*chain, 1, h)
+
+            gather_step(*chain, 1, i - lag)
+
+        @pl.when(i <= half + 1)
+        def _():
+            first_pass(i - 1)
+
         return carry
 
-    lax.fori_loop(1, half + 1, gather_slot, 0)
+    lax.fori_loop(1, half + 3, gather_slot, 0)
     for h in range(HEADS):
         top[h] = top[h] + jnp.log2(total[h])
 
@@ -352,15 +365,14 @@
         dq_t[h] += dot(key_block, dscores, 0, 0)
         return dk, dv
 
-    def second_pass(s):
+    def second_pass(s, h):
         def one(i, carry):
             pos = lax.rem(z + n_z + (1 - 2 * i) * s, n_z)
-            for h in range(HEADS):
-                key_block = kb[pos, :, h].reshape(2 * BLOCK, HEAD_SIZE)
-                value_block = vb[pos, :, h].reshape(2 * BLOCK, HEAD_SIZE)
-                dk, dv = key_terms(h, sbuf[h, pos], key_block, value_block)
-                part[0, pos, :, h] = dk.reshape(2, BLOCK, HEAD_SIZE)
-                part[1, pos, :, h] = dv.reshape(2, BLOCK, HEAD_SIZE)
+            key_block = kb[pos, :, h].reshape(2 * BLOCK, HEAD_SIZE)
+            value_block = vb[pos, :, h].reshape(2 * BLOCK, HEAD_SIZE)
+            dk, dv = key_terms(h, sbuf[h, pos], key_block, value_block)
+            part[0, pos, :, h] = dk.reshape(2, BLOCK, HEAD_SIZE)
+            part[1, pos, :, h] = dv.reshape(2, BLOCK, HEAD_SIZE)
             return carry
 
         lax.fori_loop(0, spots(s), one, 0)
@@ -381,25 +393,18 @@
     def own_term(kind, d, r, h, s):
         return part[kind, place(1 - d, s), r, h]
 
-    def sum_step(kind, s):
-        for r in (1, 0):
-            for h in range(HEADS):
-                for d in (0, 1):
-
-                    @pl.when(s == hops(d, r))
-                    def _():
-                        sb[kind, d, r, h, s] = own_term(kind, d, r, h, s).astype(BF16)
-
-                    @pl.when(s < hops(d, r))
-                    def _():
-                        sum_land(kind, d, r, h, s).wait_recv()
-                        sb[kind, d, r, h, s] = (
-                            own_term(kind, d, r, h, s) + rb[kind, d, r, h, s].astype(F32)
-                        ).astype(BF16)
-
-                    @pl.when(s <= hops(d, r))
-                    def _():
-                        sum_send(kind, d, r, h, s).start()
+    long_set = ((0, 0), (1, 1))
+    short_set = ((1, 0), (0, 1))
+
+    def sum_step(kind, pairs, s, first=False, heads=range(HEADS)):
+        for h in heads:
+            for d, r in pairs:
+                term = own_term(kind, d, r, h, s)
+                if not first:
+                    sum_land(kind, d, r, h, s).wait_recv()
+                    term = term + rb[kind, d, r, h, s].astype(F32)
+                sb[kind, d, r, h, s] = term.astype(BF16)
+                sum_send(kind, d, r, h, s).start()
 
     def arrived(kind, r, h):
         for d in (0, 1):
@@ -410,12 +415,28 @@
 
     def sum_slot(u, carry):
         s = half - u
-        second_pass(s)
-        sum_step(0, s)
+        for h in range(HEADS):
+            second_pass(s, h)
+
+            @pl.when(u == 0)
+            def _():
+                sum_step(0, long_set, s, True, (h,))
+
+            @pl.when(u == 1)
+            def _():
+                sum_step(0, short_set, s, True, (h,))
+
+            @pl.when((u > 1) & (s > 0))
+            def _():
+                sum_step(0, short_set, s, False, (h,))
+
+        @pl.when((u > 0) & (s > 0))
+        def _():
+            sum_step(0, long_set, s)
+
         return carry
 
-    lax.fori_loop(0, half, sum_slot, 0)
-    second_pass(0)
+    lax.fori_loop(0, half + 1, sum_slot, 0)
 
     def swap(kind, r, h):
         yb[kind, r, h, 0] = arrived(kind, r, h).astype(BF16)
@@ -426,15 +447,18 @@
 
     swaps = {}
     for h in range(HEADS):
-        for r in (1, 0):
-            swaps[0, r, h] = swap(0, r, h)
-    sum_step(1, half)
+        swaps[0, 1, h] = swap(0, 1, h)
+    sum_step(1, long_set, half, True)
 
     for h in range(HEADS):
         lanes = slice(h * 128, (h + 1) * 128)
         dk, dv = key_terms(h, sc[h], kvc[0, :, lanes], kvc[1, :, lanes])
         gkvc[0, :, lanes] = dk.astype(BF16)
         gkvc[1, :, lanes] = dv.astype(BF16)
+
+    sum_step(1, short_set, half - 1, True)
+    for h in range(HEADS):
+        swaps[0, 0, h] = swap(0, 0, h)
 
     for h in range(HEADS):
         for j in range(GROUP):
@@ -458,7 +482,7 @@
         near.start()
         far.start()
 
-    sum_step(1, half - 1)
+    sum_step(1, long_set, half - 1)
     copies[9].wait()
     lands[9].wait_recv()
     proj[...] = jnp.zeros(proj.shape, F32)
@@ -482,6 +506,8 @@
             gather_start(*grads, r, h)
             if r == 0:
                 give_prompt(3 + h, dkb.at[z, 0, h], gpk_out, h)
+        if r == 0:
+            sum_step(1, short_set, half - 2)
 
     def project(h, s):
         def one(i, carry):
@@ -530,30 +556,41 @@
                 def _():
                     proj_send(i_st, t).start()
 
+    def value_final():
+        for h in range(HEADS):
+            yb[1, 1, h, 0] = arrived(1, 1, h).astype(BF16)
+            i = 4 + 3 * HEADS + h
+            crossing = across(yb.at[1, 1, h, 0], yb.at[1, 0, h, 1], i)
+            crossing.start()
+            swaps[1, 0, h] = (crossing, across(yb.at[1, 0, h, 1], yb.at[1, 0, h, 1], i))
+
+    rest = []
+    for s in range(half - 2, 0, -1):
+        rest.append((long_set, s))
+        if s > 1:
+            rest.append((short_set, s - 1))
+    when = {0: (), 1: rest[:1], 2: rest[1:], 3: ()} if half > 3 else {half - 1: rest}
+
     for h in range(HEADS):
         project(h, 0)
     for s in range(1, half):
-        for h in range(HEADS):
-            gather_step(*grads, s, (h,))
+        gather_step(*grads, 0, s)
+        gather_step(*grads, 1, s)
+        for pairs, at in when.get(s, ()):
+            sum_step(1, pairs, at)
+        if s == half - 1:
+            value_final()
         for h in range(HEADS):
             project(h, s)
     for h in range(HEADS):
-        gather_step(*grads, half, (h,))
+        for r in (0, 1):
+            gather_step(*grads, r, half, (h,))
         project(h, half)
         scatter(h)
 
     @pl.when(src_core == core)
     def _():
         prx[g] = pack[0, g - core * per_core]
-
-    for s in range(half - 2, 0, -1):
-        sum_step(1, s)
-    for h in range(HEADS):
-        yb[1, 1, h, 0] = arrived(1, 1, h).astype(BF16)
-        i = 4 + 3 * HEADS + h
-        crossing = across(yb.at[1, 1, h, 0], yb.at[1, 0, h, 1], i)
-        crossing.start()
-        swaps[1, 0, h] = (crossing, across(yb.at[1, 0, h, 1], yb.at[1, 0, h, 1], i))
 
     def collect(i, acc):
         @pl.when(jnp.logical_or(src_ctx != c, i != g))

time: 103 us -> 97.7 us (0.949)
  Pallas kernels: 102 us -> 96.9 us
    pallas_call x1, Pallas kernels: 99.8 us -> 95 us  [body(): pl.pallas_call(functools.partial(kernel, n_z, n_dp), out_shape=[jax.Shape...]
where the time goes in v3:
time: 97.7 us; the launch traced here: 97.5 us
  Pallas kernels  96.9 us (99%)
    pallas_call x1, Pallas kernels, body(): pl.pallas_call(functools.partial(kernel, n_z, n_dp), out_shape=[jax.Shape...  95 us

profile of v3, /device:TPU:1, one launch (start us, length us, event | category | flops | bytes accessed | tf_op | source)
XLA Modules:
  0.0 97.5 jit_solution(12261628077440478232)
XLA Ops:
  0.6 95.0 %shard_map.136 = (bf16[64,2560]{1,0:T(8,128)(2,1)}, bf16[64,512]{1,0:T(8,128)(2,1)}, bf16[64,512]{1,0:T(8,128)(2,1)}, bf16[64,512]{1,0:T(8,128)(2,1)}, bf16[64,512]{1,0:T(8,128)(2,1)}, /*index=5*/f32[32,160]{1,0:T(8,128)}) custom-call(bf16[64,2560]{1,0:T(8,128)(2,1)} %bitcast.18, bf16[64,2560]{1,0:T(8,128)(2,1)} %bitcast.19, bf16[64,2560]{1,0:T(8,128)(2,1)} %bitcast.20, ...), custom_call_target="tpu_custom_call" | custom-call | tf_op jit(solution)/shard_map/pallas_call | solution.py:663
  95.7 1.9 %shard_map.137 = (bf16[64,2560]{1,0:T(8,128)(2,1)}, bf16[64,512]{1,0:T(8,128)(2,1)}, bf16[64,512]{1,0:T(8,128)(2,1)}, bf16[64,512]{1,0:T(8,128)(2,1)}, bf16[64,512]{1,0:T(8,128)(2,1)}, /*index=5*/f32[32,160]{1,0:T(8,128)}) custom-call(bf16[64,2560]{1,0:T(8,128)(2,1)} %get-tuple-element.18.refs_0_, bf16[64,512]{1,0:T(8,128)(2,1)} %get-tuple-element.19.refs_1_, ...), custom_call_target="tpu_custom_call" | custom-call | tf_op jit(solution)/shard_map/pallas_call | solution.py:722

commit v4 on v3

--- a/solution.py
+++ b/solution.py
@@ -578,10 +578,10 @@
         gather_step(*grads, 1, s)
         for pairs, at in when.get(s, ()):
             sum_step(1, pairs, at)
+        for h in range(HEADS):
+            project(h, s)
         if s == half - 1:
             value_final()
-        for h in range(HEADS):
-            project(h, s)
     for h in range(HEADS):
         for r in (0, 1):
             gather_step(*grads, r, half, (h,))

time: 97.7 us -> 97.9 us (level)
  no operation moved by 1% of the time
where the time goes in v4:
time: 97.9 us; the launch traced here: 97.8 us
  Pallas kernels  97.1 us (99%)
    pallas_call x1, Pallas kernels, body(): pl.pallas_call(functools.partial(kernel, n_z, n_dp), out_shape=[jax.Shape...  95.2 us

profile of v4, /device:TPU:1, one launch (start us, length us, event | category | flops | bytes accessed | tf_op | source)
XLA Modules:
  0.0 97.8 jit_solution(13469299362160192795)
XLA Ops:
  0.6 95.2 %shard_map.136 = (bf16[64,2560]{1,0:T(8,128)(2,1)}, bf16[64,512]{1,0:T(8,128)(2,1)}, bf16[64,512]{1,0:T(8,128)(2,1)}, bf16[64,512]{1,0:T(8,128)(2,1)}, bf16[64,512]{1,0:T(8,128)(2,1)}, /*index=5*/f32[32,160]{1,0:T(8,128)}) custom-call(bf16[64,2560]{1,0:T(8,128)(2,1)} %bitcast.18, bf16[64,2560]{1,0:T(8,128)(2,1)} %bitcast.19, bf16[64,2560]{1,0:T(8,128)(2,1)} %bitcast.20, ...), custom_call_target="tpu_custom_call" | custom-call | tf_op jit(solution)/shard_map/pallas_call | solution.py:663
  95.9 1.9 %shard_map.137 = (bf16[64,2560]{1,0:T(8,128)(2,1)}, bf16[64,512]{1,0:T(8,128)(2,1)}, bf16[64,512]{1,0:T(8,128)(2,1)}, bf16[64,512]{1,0:T(8,128)(2,1)}, bf16[64,512]{1,0:T(8,128)(2,1)}, /*index=5*/f32[32,160]{1,0:T(8,128)}) custom-call(bf16[64,2560]{1,0:T(8,128)(2,1)} %get-tuple-element.18.refs_0_, bf16[64,512]{1,0:T(8,128)(2,1)} %get-tuple-element.19.refs_1_, ...), custom_call_target="tpu_custom_call" | custom-call | tf_op jit(solution)/shard_map/pallas_call | solution.py:722
